TPU v7x, 512 devices: a whole 4x4x16 slice. The times are simulated.
512 devices in a mesh: ctx: 16 (over z_lo, x), tp: 32 (over y, z_hi, core).
Axes of the slice: x: 4, y: 4, z: 16 (z_hi: 4, z_lo: 4; z = z_hi * 4 + z_lo), core: 2. Of those that a mesh axis runs over, the one named last changes fastest.
Arguments:
- query_act: bfloat16 [8192, 4096], P('ctx', 'tp'), may hold values from -6 to 6
- key_act: bfloat16 [8192, 4096], P('ctx', 'tp'), may hold values from -6 to 6
- value_act: bfloat16 [8192, 4096], P('ctx', 'tp'), may hold values from -6 to 6
- filter_taps: float32 [8192, 128], P('ctx'), may hold values from -0.06629126 to 0.06629126
- cotangent: bfloat16 [8192, 4096], P('ctx', 'tp'), may hold values from -6 to 6
Outputs:
- gated_out: bfloat16 [8192, 4096], P('ctx', 'tp')
- grad_query: bfloat16 [8192, 4096], P('ctx', 'tp')
- grad_key: bfloat16 [8192, 4096], P('ctx', 'tp')
- grad_value: bfloat16 [8192, 4096], P('ctx', 'tp')
- grad_filter: float32 [8192, 128], P('ctx')
All inputs are finite; a program needn't handle non-finite values.
Results may differ from a plain program's by a relative error of at most 0.001.
Values sent between devices are 32-bit elements; how exact they have to be, the bound alone decides.
No kernel may reach another device: no remote copies, remote signals or barrier semaphores. Data moves between devices by JAX's collectives and lax.ppermute only.
A program may use at most 64 MiB of HBM per device.

v0:
```python
import math

import jax
import jax.numpy as jnp
from jax import lax
from jax.sharding import PartitionSpec as P

BLOCK = 4


PRECISE = lax.Precision.HIGHEST


def phase_table(row_count, column_count, full_len, row_start, column_start):
    row_numbers = row_start + lax.iota(jnp.int32, row_count)
    column_numbers = column_start + lax.iota(jnp.int32, column_count)
    product = row_numbers[:, None] * column_numbers[None, :] % full_len
    phase_angle = product.astype(jnp.float32) * (2.0 * math.pi / full_len)
    return (jnp.cos(phase_angle), jnp.sin(phase_angle))


def spread_forward(signal):
    pieces = lax.axis_size("ctx")
    stack_size, row_count, channel_count = signal.shape
    second_len = row_count // BLOCK
    first_len = 2 * pieces * BLOCK
    full_len = first_len * second_len
    share_len = second_len // pieces
    arranged = signal.reshape(stack_size, BLOCK, second_len, channel_count)
    columns = lax.all_to_all(arranged, "ctx", split_axis=2, concat_axis=1, tiled=True)
    cosine_first, sine_first = phase_table(first_len, pieces * BLOCK, first_len, 0, 0)
    part_real = jnp.einsum("kn,gnbc->gkbc", cosine_first, columns, precision=PRECISE)
    part_imag = -jnp.einsum("kn,gnbc->gkbc", sine_first, columns, precision=PRECISE)
    cosine_twist, sine_twist = phase_table(
        first_len, share_len, full_len, 0, lax.axis_index("ctx") * share_len
    )
    cosine_twist = cosine_twist[None, :, :, None]
    sine_twist = sine_twist[None, :, :, None]
    part_real, part_imag = (
        part_real * cosine_twist + part_imag * sine_twist,
        part_imag * cosine_twist - part_real * sine_twist,
    )
    part_real, part_imag = (
        lax.all_to_all(part_real, "ctx", split_axis=1, concat_axis=2, tiled=True),
        lax.all_to_all(part_imag, "ctx", split_axis=1, concat_axis=2, tiled=True),
    )
    cosine_second, sine_second = phase_table(second_len, second_len, second_len, 0, 0)
    spec_real = jnp.einsum(
        "kn,gjnc->gjkc", cosine_second, part_real, precision=PRECISE
    ) + jnp.einsum("kn,gjnc->gjkc", sine_second, part_imag, precision=PRECISE)
    spec_imag = jnp.einsum(
        "kn,gjnc->gjkc", cosine_second, part_imag, precision=PRECISE
    ) - jnp.einsum("kn,gjnc->gjkc", sine_second, part_real, precision=PRECISE)
    return (spec_real, spec_imag)


def spread_inverse(spec_real, spec_imag):
    pieces = lax.axis_size("ctx")
    stack_size, share_len, second_len, channel_count = spec_real.shape
    first_len = share_len * pieces
    full_len = first_len * second_len
    cosine_second, sine_second = phase_table(second_len, second_len, second_len, 0, 0)
    part_real = jnp.einsum(
        "nk,gjkc->gjnc", cosine_second, spec_real, precision=PRECISE
    ) - jnp.einsum("nk,gjkc->gjnc", sine_second, spec_imag, precision=PRECISE)
    part_imag = jnp.einsum(
        "nk,gjkc->gjnc", cosine_second, spec_imag, precision=PRECISE
    ) + jnp.einsum("nk,gjkc->gjnc", sine_second, spec_real, precision=PRECISE)
    cosine_twist, sine_twist = phase_table(
        share_len, second_len, full_len, lax.axis_index("ctx") * share_len, 0
    )
    cosine_twist = cosine_twist[None, :, :, None]
    sine_twist = sine_twist[None, :, :, None]
    part_real, part_imag = (
        part_real * cosine_twist - part_imag * sine_twist,
        part_imag * cosine_twist + part_real * sine_twist,
    )
    part_real, part_imag = (
        lax.all_to_all(part_real, "ctx", split_axis=2, concat_axis=1, tiled=True),
        lax.all_to_all(part_imag, "ctx", split_axis=2, concat_axis=1, tiled=True),
    )
    cosine_first, sine_first = phase_table(pieces * BLOCK, first_len, first_len, 0, 0)
    samples = (
        jnp.einsum("nk,gkbc->gnbc", cosine_first, part_real, precision=PRECISE)
        - jnp.einsum("nk,gkbc->gnbc", sine_first, part_imag, precision=PRECISE)
    ) / full_len
    row_blocks = lax.all_to_all(samples, "ctx", split_axis=1, concat_axis=2, tiled=True)
    return row_blocks.reshape(stack_size, BLOCK * second_len * pieces // pieces, channel_count)


def on_device(query_act, key_act, value_act, filter_taps, cotangent):
    forward_fn, inverse_fn = (spread_forward, spread_inverse)
    query_rows = query_act.astype(jnp.float32)
    key_rows = key_act.astype(jnp.float32)
    value_rows = value_act.astype(jnp.float32)
    grad_rows = cotangent.astype(jnp.float32)
    gate_in = key_rows * value_rows
    spec_real, spec_imag = forward_fn(jnp.stack([gate_in, filter_taps]))
    gate_real, filter_real = (spec_real[0], spec_real[1])
    gate_imag, filter_imag = (spec_imag[0], spec_imag[1])
    mixed_real = filter_real * gate_real - filter_imag * gate_imag
    mixed_imag = filter_real * gate_imag + filter_imag * gate_real
    conv_out = inverse_fn(mixed_real[None], mixed_imag[None])[0]
    gated_out = (query_rows * conv_out).astype(jnp.bfloat16)
    grad_query = (grad_rows * conv_out).astype(jnp.bfloat16)
    grad_conv = grad_rows * query_rows
    grad_real, grad_imag = forward_fn(grad_conv[None])
    grad_real = grad_real[0]
    grad_imag = grad_imag[0]
    back_real = jnp.stack(
        [
            filter_real * grad_real + filter_imag * grad_imag,
            gate_real * grad_real + gate_imag * grad_imag,
        ]
    )
    back_imag = jnp.stack(
        [
            filter_real * grad_imag - filter_imag * grad_real,
            gate_real * grad_imag - gate_imag * grad_real,
        ]
    )
    both = inverse_fn(back_real, back_imag)
    grad_gate = both[0]
    filter_terms = both[1]
    grad_key = (grad_gate * value_rows).astype(jnp.bfloat16)
    grad_value = (grad_gate * key_rows).astype(jnp.bfloat16)
    summed = lax.psum(filter_terms, "tp")
    scale_count = lax.axis_size("ctx") * query_act.shape[0] * lax.axis_size("tp")
    grad_filter = summed / math.sqrt(float(scale_count))
    return (gated_out, grad_query, grad_key, grad_value, grad_filter)


def solution(mesh):
    return jax.shard_map(
        on_device,
        mesh=mesh,
        in_specs=(P("ctx", "tp"), P("ctx", "tp"), P("ctx", "tp"), P("ctx", None), P("ctx", "tp")),
        out_specs=(P("ctx", "tp"), P("ctx", "tp"), P("ctx", "tp"), P("ctx", "tp"), P("ctx", None)),
        check_vma=False,
    )
```

profile of v0, /device:TPU:1, one launch (start us, length us, event | category | flops | bytes accessed | tf_op | source)
XLA Modules:
  0.0 637.9 jit_solution(5147987865851650458)
XLA Ops:
  7.2 1.0 convert_multiply_fusion
  8.2 0.9 copy.110
  9.0 9.1 %all-to-all-start.6 = ((f32[1,4,128,128]{3,1,0,2:T(4,128)}), f32[1,4,128,128]{3,1,0,2:T(4,128)S(1)}, u32[]{:S(2)}, u32[]{:S(2)}) async-start(f32[1,4,128,128]{3,1,0,2:T(4,128)} %copy.110), calls=%async_computation.6 | async-start | bytes 524288 | tf_op jit(solution)/shard_map/all_to_all | solution.py:30
  18.3 0.9 copy-done.9
  19.2 1.2 copy.89
  20.4 6.9 %all-to-all-done.6 = f32[1,4,128,128]{3,1,0,2:T(4,128)S(1)} async-done(((f32[1,4,128,128]{3,1,0,2:T(4,128)}), f32[1,4,128,128]{3,1,0,2:T(4,128)S(1)}, u32[]{:S(2)}, u32[]{:S(2)}) %all-to-all-start.6) | async-done | bytes 262176 | tf_op jit(solution)/shard_map/all_to_all | solution.py:30
  27.3 4.6 all-to-all-start
  32.2 1.0 fusion.5
  33.2 1.0 multiply_subtract_fusion.3
  34.3 1.0 copy.113
  35.2 9.8 %all-to-all-done = f32[2,4,128,128]{3,1,0,2:T(4,128)S(1)} async-done(((f32[2,4,128,128]{3,1,0,2:T(4,128)}), f32[2,4,128,128]{3,1,0,2:T(4,128)S(1)}, u32[]{:S(2)}, u32[]{:S(2)}) %all-to-all-start) | async-done | bytes 524320 | tf_op jit(solution)/shard_map/all_to_all | solution.py:30
  45.0 5.6 all-to-all-start.7
  50.6 1.0 copy.116
  51.7 11.7 %all-to-all-done.7 = f32[1,128,8,128]{3,2,0,1:T(8,128)S(1)} async-done(((f32[1,128,8,128]{3,2,0,1:T(8,128)}), f32[1,128,8,128]{3,2,0,1:T(8,128)S(1)}, u32[]{:S(2)}, u32[]{:S(2)}) %all-to-all-start.7) | async-done | bytes 524320 | tf_op jit(solution)/shard_map/all_to_all | solution.py:44
  63.4 5.6 all-to-all-start.8
  69.5 1.8 convolution_bitcast_fusion
  71.3 1.8 multiply_add_fusion
  73.1 1.4 copy.92
  74.5 6.8 %all-to-all-done.8 = f32[1,128,8,128]{3,2,0,1:T(8,128)S(1)} async-done(((f32[1,128,8,128]{3,2,0,1:T(8,128)}), f32[1,128,8,128]{3,2,0,1:T(8,128)S(1)}, u32[]{:S(2)}, u32[]{:S(2)}) %all-to-all-start.8) | async-done | bytes 524320 | tf_op jit(solution)/shard_map/all_to_all | solution.py:45
  81.3 6.2 all-to-all-start.1
  87.5 1.4 copy.96
  88.9 20.7 %all-to-all-done.1 = f32[2,128,8,128]{3,2,0,1:T(8,128)S(1)} async-done(((f32[2,128,8,128]{3,2,0,1:T(8,128)}), f32[2,128,8,128]{3,2,0,1:T(8,128)S(1)}, u32[]{:S(2)}, u32[]{:S(2)}) %all-to-all-start.1) | async-done | bytes 1048608 | tf_op jit(solution)/shard_map/all_to_all | solution.py:44
  109.6 8.2 %all-to-all-start.2 = ((f32[2,128,8,128]{3,2,0,1:T(8,128)}), f32[2,128,8,128]{3,2,0,1:T(8,128)S(1)}, u32[]{:S(2)}, u32[]{:S(2)}) async-start(f32[2,128,8,128]{3,2,0,1:T(8,128)} %copy.96), calls=%async_computation.2 | async-start | bytes 2097152 | tf_op jit(solution)/shard_map/all_to_all | solution.py:45
  117.9 1.1 fusion.33
  119.1 1.9 fusion.7
  121.0 1.9 fusion.29
  122.9 2.9 fusion.21
  125.8 13.6 %all-to-all-done.2 = f32[2,128,8,128]{3,2,0,1:T(8,128)S(1)} async-done(((f32[2,128,8,128]{3,2,0,1:T(8,128)}), f32[2,128,8,128]{3,2,0,1:T(8,128)S(1)}, u32[]{:S(2)}, u32[]{:S(2)}) %all-to-all-start.2) | async-done | bytes 1048608 | tf_op jit(solution)/shard_map/all_to_all | solution.py:45
  139.5 1.9 fusion.17
  141.4 1.9 fusion.2
  143.4 1.9 fusion.1
  145.4 1.5 multiply_add_fusion.2
  148.5 0.8 fusion.8
  149.3 0.9 add_bitcast_fusion.1
  150.2 1.0 copy.102
  151.2 7.8 %all-to-all-start.3 = ((f32[1,8,128,128]{3,1,0,2:T(8,128)}), f32[1,8,128,128]{3,1,0,2:T(8,128)S(1)}, u32[]{:S(2)}, u32[]{:S(2)}) async-start(f32[1,8,128,128]{3,1,0,2:T(8,128)} %copy.102), calls=%async_computation.3 | async-start | bytes 1048576 | tf_op jit(solution)/shard_map/all_to_all | solution.py:79
  159.0 1.0 copy.105
  160.0 12.1 %all-to-all-done.3 = f32[1,8,128,128]{3,1,0,2:T(8,128)S(1)} async-done(((f32[1,8,128,128]{3,1,0,2:T(8,128)}), f32[1,8,128,128]{3,1,0,2:T(8,128)S(1)}, u32[]{:S(2)}, u32[]{:S(2)}) %all-to-all-start.3) | async-done | bytes 524320 | tf_op jit(solution)/shard_map/all_to_all | solution.py:79
  172.1 0.8 copy-done.1
  172.9 5.5 all-to-all-start.4
  178.4 1.2 fusion.28
  179.7 1.2 fusion.27
  180.9 1.2 convolution_add_fusion
  182.1 1.4 add_bitcast_fusion
  183.5 1.4 copy.121
  184.9 6.1 all-to-all-done.4
  191.0 6.0 all-to-all-start.9
  197.0 1.4 copy.124
  198.4 20.7 %all-to-all-done.9 = f32[2,8,128,128]{3,1,0,2:T(8,128)S(1)} async-done(((f32[2,8,128,128]{3,1,0,2:T(8,128)}), f32[2,8,128,128]{3,1,0,2:T(8,128)S(1)}, u32[]{:S(2)}, u32[]{:S(2)}) %all-to-all-start.9) | async-done | bytes 1048608 | tf_op jit(solution)/shard_map/all_to_all | solution.py:79
  219.1 8.0 %all-to-all-start.10 = ((f32[2,8,128,128]{3,1,0,2:T(8,128)}), f32[2,8,128,128]{3,1,0,2:T(8,128)S(1)}, u32[]{:S(2)}, u32[]{:S(2)}) async-start(f32[2,8,128,128]{3,1,0,2:T(8,128)} %copy.124), calls=%async_computation.10 | async-start | bytes 2097152 | tf_op jit(solution)/shard_map/all_to_all | solution.py:80
  227.2 1.1 copy.203
  229.9 0.9 copy.108
  230.8 18.4 %all-to-all-done.10 = f32[2,8,128,128]{3,1,0,2:T(8,128)S(1)} async-done(((f32[2,8,128,128]{3,1,0,2:T(8,128)}), f32[2,8,128,128]{3,1,0,2:T(8,128)S(1)}, u32[]{:S(2)}, u32[]{:S(2)}) %all-to-all-start.10) | async-done | bytes 1048608 | tf_op jit(solution)/shard_map/all_to_all | solution.py:80
  249.2 7.8 %all-to-all-start.5 = ((f32[1,64,8,128]{3,2,0,1:T(8,128)}), f32[1,64,8,128]{3,2,0,1:T(8,128)S(1)}, u32[]{:S(2)}, u32[]{:S(2)}) async-start(f32[1,64,8,128]{3,2,0,1:T(8,128)} %copy.108), calls=%async_computation.5 | async-start | bytes 524288 | tf_op jit(solution)/shard_map/all_to_all | solution.py:87
  257.0 0.8 fusion.14
  257.8 0.8 fusion.4
  258.6 1.1 copy.127
  259.7 6.1 all-to-all-done.5
  265.8 4.4 all-to-all-start.11
  270.3 12.6 %all-to-all-done.11 = f32[2,64,8,128]{3,2,0,1:T(8,128)S(1)} async-done(((f32[2,64,8,128]{3,2,0,1:T(8,128)}), f32[2,64,8,128]{3,2,0,1:T(8,128)S(1)}, u32[]{:S(2)}, u32[]{:S(2)}) %all-to-all-start.11) | async-done | bytes 524320 | tf_op jit(solution)/shard_map/all_to_all | solution.py:87
  283.7 0.9 copy-done.6
  284.6 0.8 fusion.51
  285.5 343.7 %all-reduce.2.cloned.1.call-done = f32[512,128]{1,0:T(8,128)} async-done(((f32[512,128]{1,0:T(8,128)}), f32[512,128]{1,0:T(8,128)}) %all-reduce.2.cloned.1.call-update) | async-done | bytes 262160 | tf_op jit(solution)/shard_map/psum | solution.py:127
  629.1 1.7 broadcast_multiply_fusion
  (36 shorter events, 5.2 us)
Async XLA Ops:
  9.0 9.2 %copy-start.5 = (bf16[512,128]{1,0:T(8,128)(2,1)S(1)}, bf16[512,128]{1,0:T(8,128)(2,1)}, u32[]{:S(2)}) copy-start(bf16[512,128]{1,0:T(8,128)(2,1)} %param.6) | copy-start | bytes 393220
  9.0 9.2 %copy-start.8 = (bf16[512,128]{1,0:T(8,128)(2,1)S(1)}, bf16[512,128]{1,0:T(8,128)(2,1)}, u32[]{:S(2)}) copy-start(bf16[512,128]{1,0:T(8,128)(2,1)} %param.7) | copy-start | bytes 393220
  9.0 18.2 %all-to-all-start.6 = ((f32[1,4,128,128]{3,1,0,2:T(4,128)}), f32[1,4,128,128]{3,1,0,2:T(4,128)S(1)}, u32[]{:S(2)}, u32[]{:S(2)}) async-start(f32[1,4,128,128]{3,1,0,2:T(4,128)} %copy.110), calls=%async_computation.6 | async-start | bytes 524288 | tf_op jit(solution)/shard_map/all_to_all | solution.py:30
  18.2 1.0 copy-start.9
  27.3 17.8 %all-to-all-start = ((f32[2,4,128,128]{3,1,0,2:T(4,128)}), f32[2,4,128,128]{3,1,0,2:T(4,128)S(1)}, u32[]{:S(2)}, u32[]{:S(2)}) async-start(f32[2,4,128,128]{3,1,0,2:T(4,128)} %copy.89), calls=%async_computation | async-start | bytes 1048576 | tf_op jit(solution)/shard_map/all_to_all | solution.py:30
  45.0 18.3 %all-to-all-start.7 = ((f32[1,128,8,128]{3,2,0,1:T(8,128)}), f32[1,128,8,128]{3,2,0,1:T(8,128)S(1)}, u32[]{:S(2)}, u32[]{:S(2)}) async-start(f32[1,128,8,128]{3,2,0,1:T(8,128)} %copy.113), calls=%async_computation.7 | async-start | bytes 1048576 | tf_op jit(solution)/shard_map/all_to_all | solution.py:44
  63.4 18.0 %all-to-all-start.8 = ((f32[1,128,8,128]{3,2,0,1:T(8,128)}), f32[1,128,8,128]{3,2,0,1:T(8,128)S(1)}, u32[]{:S(2)}, u32[]{:S(2)}) async-start(f32[1,128,8,128]{3,2,0,1:T(8,128)} %copy.116), calls=%async_computation.8 | async-start | bytes 1048576 | tf_op jit(solution)/shard_map/all_to_all | solution.py:45
  81.3 28.3 %all-to-all-start.1 = ((f32[2,128,8,128]{3,2,0,1:T(8,128)}), f32[2,128,8,128]{3,2,0,1:T(8,128)S(1)}, u32[]{:S(2)}, u32[]{:S(2)}) async-start(f32[2,128,8,128]{3,2,0,1:T(8,128)} %copy.92), calls=%async_computation.1 | async-start | bytes 2097152 | tf_op jit(solution)/shard_map/all_to_all | solution.py:44
  109.6 29.9 %all-to-all-start.2 = ((f32[2,128,8,128]{3,2,0,1:T(8,128)}), f32[2,128,8,128]{3,2,0,1:T(8,128)S(1)}, u32[]{:S(2)}, u32[]{:S(2)}) async-start(f32[2,128,8,128]{3,2,0,1:T(8,128)} %copy.96), calls=%async_computation.2 | async-start | bytes 2097152 | tf_op jit(solution)/shard_map/all_to_all | solution.py:45
  139.5 1.9 copy-start
  143.4 2.0 copy-start.3
  143.4 2.0 copy-start.4
  151.2 20.9 %all-to-all-start.3 = ((f32[1,8,128,128]{3,1,0,2:T(8,128)}), f32[1,8,128,128]{3,1,0,2:T(8,128)S(1)}, u32[]{:S(2)}, u32[]{:S(2)}) async-start(f32[1,8,128,128]{3,1,0,2:T(8,128)} %copy.102), calls=%async_computation.3 | async-start | bytes 1048576 | tf_op jit(solution)/shard_map/all_to_all | solution.py:79
  172.1 0.8 copy-start.1
  172.9 18.1 %all-to-all-start.4 = ((f32[1,8,128,128]{3,1,0,2:T(8,128)}), f32[1,8,128,128]{3,1,0,2:T(8,128)}, u32[]{:S(2)}, u32[]{:S(2)}) async-start(f32[1,8,128,128]{3,1,0,2:T(8,128)} %copy.105), calls=%async_computation.4 | async-start | bytes 1048576 | tf_op jit(solution)/shard_map/all_to_all | solution.py:80
  191.0 28.1 %all-to-all-start.9 = ((f32[2,8,128,128]{3,1,0,2:T(8,128)}), f32[2,8,128,128]{3,1,0,2:T(8,128)S(1)}, u32[]{:S(2)}, u32[]{:S(2)}) async-start(f32[2,8,128,128]{3,1,0,2:T(8,128)} %copy.121), calls=%async_computation.9 | async-start | bytes 2097152 | tf_op jit(solution)/shard_map/all_to_all | solution.py:79
  198.4 28.7 %copy-start.2 = (f32[1,8,128,128]{3,1,0,2:T(8,128)S(1)}, f32[1,8,128,128]{3,1,0,2:T(8,128)}, u32[]{:S(2)}) copy-start(f32[1,8,128,128]{3,1,0,2:T(8,128)} %copy-done.1) | copy-start | bytes 1572868
  219.1 30.1 %all-to-all-start.10 = ((f32[2,8,128,128]{3,1,0,2:T(8,128)}), f32[2,8,128,128]{3,1,0,2:T(8,128)S(1)}, u32[]{:S(2)}, u32[]{:S(2)}) async-start(f32[2,8,128,128]{3,1,0,2:T(8,128)} %copy.124), calls=%async_computation.10 | async-start | bytes 2097152 | tf_op jit(solution)/shard_map/all_to_all | solution.py:80
  249.2 16.6 %all-to-all-start.5 = ((f32[1,64,8,128]{3,2,0,1:T(8,128)}), f32[1,64,8,128]{3,2,0,1:T(8,128)S(1)}, u32[]{:S(2)}, u32[]{:S(2)}) async-start(f32[1,64,8,128]{3,2,0,1:T(8,128)} %copy.108), calls=%async_computation.5 | async-start | bytes 524288 | tf_op jit(solution)/shard_map/all_to_all | solution.py:87
  265.8 17.1 %all-to-all-start.11 = ((f32[2,64,8,128]{3,2,0,1:T(8,128)}), f32[2,64,8,128]{3,2,0,1:T(8,128)S(1)}, u32[]{:S(2)}, u32[]{:S(2)}) async-start(f32[2,64,8,128]{3,2,0,1:T(8,128)} %copy.127), calls=%async_computation.11 | async-start | bytes 1048576 | tf_op jit(solution)/shard_map/all_to_all | solution.py:87
  270.2 358.9 %all-reduce.2.cloned.1.call-start = ((), (), s32[]{:S(2)}) async-start(), calls=%async_computation.12 | async-start | bytes 524288 | tf_op jit(solution)/shard_map/psum | solution.py:127
  283.6 0.9 copy-start.6
  283.7 1.0 copy-start.7
Sparse Core Ops, SparseCore 0:
  283.8 345.2 all-reduce.1
where the time goes:
time: 646 us; the launch traced here: 638 us
  waiting for transfers between devices  489 us (76%)
  starting transfers between devices  78.9 us (12%)
  matrix products  32.4 us (5%)
  local copies, waits for them, and re-layouts  18.9 us (3%)
  between operations  14.7 us (2%)
    psum x1, waiting for transfers between devices, on_device(): summed = lax.psum(filter_terms, 'tp')  344 us
    all_to_all x2, waiting for transfers between devices, spread_inverse(): lax.all_to_all(part_real, 'ctx', split_axis=2, concat_axis=1, tiled=True)  32.7 us
    all_to_all x2, waiting for transfers between devices, spread_forward(): lax.all_to_all(part_real, 'ctx', split_axis=1, concat_axis=2, tiled=True)  32.4 us
    all_to_all x2, waiting for transfers between devices, spread_inverse(): lax.all_to_all(part_imag, 'ctx', split_axis=2, concat_axis=1, tiled=True)  24.5 us
    all_to_all x2, waiting for transfers between devices, spread_forward(): lax.all_to_all(part_imag, 'ctx', split_axis=1, concat_axis=2, tiled=True)  20.4 us
    all_to_all x2, waiting for transfers between devices, spread_inverse(): lax.all_to_all(samples, 'ctx', split_axis=1, concat_axis=2, tiled=True)  18.6 us
    all_to_all x2, waiting for transfers between devices, spread_forward(): lax.all_to_all(arranged, 'ctx', split_axis=2, concat_axis=1, tiled=True)  16.7 us
    all_to_all x2, starting transfers between devices, spread_forward(): lax.all_to_all(part_imag, 'ctx', split_axis=1, concat_axis=2, tiled=True)  13.9 us
  transfers between devices with their start and end apart: 13, of which 13 were waited for; matrix products, arithmetic and copies ran while one was open for 6% of the time, Pallas kernels for 0%

commit v1 on v0

v1 whole, which is shorter than its diff:
```python
import math

import numpy as np
import ml_dtypes
import jax
import jax.numpy as jnp
from jax import lax
from jax.experimental import pallas as pl
from jax.experimental.pallas import tpu as pltpu
from jax.sharding import Mesh, PartitionSpec as P

LANES = 128
GROUP = ("ctx", "y", "core")
PAIRS_NEAR = [(0, 1), (1, 0), (2, 3), (3, 2)]
PAIRS_ROUND = [(0, 3), (3, 0), (1, 2), (2, 1)]


def split_const(table):
    high = table.astype(ml_dtypes.bfloat16)
    low = (table - high.astype(np.float64)).astype(ml_dtypes.bfloat16)
    return high, low


def dft_tables(blocks, chunks):
    first = blocks * chunks
    full = first * LANES
    order = (np.arange(blocks)[None, :] * chunks + np.arange(chunks)[:, None]).reshape(-1)
    k1 = np.arange(first)
    n2 = np.arange(LANES)
    angle = -2 * np.pi * (k1[:, None] * order[None, :] % first) / first + np.pi * order[None, :] / (2 * first)
    first_fwd = np.concatenate([np.cos(angle), np.sin(angle)], 0)
    high, low = split_const(first_fwd)
    first_fwd = np.concatenate([high, high, low], 1)
    high, low = split_const(np.concatenate([np.cos(angle).T, np.sin(angle).T], 1) / full)
    first_inv = np.concatenate([high, high, low], 1)
    angle = -2 * np.pi * (k1[:, None] * n2[None, :]) / full + np.pi * n2[None, :] / (2 * full)
    twist = np.concatenate([np.cos(angle), np.sin(angle)], 1).astype(np.float32)
    angle = 2 * np.pi * (n2[:, None] * n2[None, :] % LANES) / LANES
    cosine, sine = np.cos(angle), np.sin(angle)
    second = np.block([[cosine, -sine], [sine, cosine]])
    second_fwd = np.concatenate(split_const(second), 0)
    second_inv = np.concatenate(split_const(second.T), 0)
    return first_fwd, twist, second_fwd, second_inv, first_inv


def split(values):
    high = values.astype(jnp.bfloat16)
    return high, (values - high.astype(jnp.float32)).astype(jnp.bfloat16)


def dot(left, right):
    return jnp.dot(left, right, preferred_element_type=jnp.float32)


def second_stage(high, low, table):
    table_high = table[: 2 * LANES, :]
    table_low = table[2 * LANES :, :]
    return dot(high, table_high) + dot(low, table_high) + dot(high, table_low)


def pack_kernel(chunks, place_ref, query_ref, key_ref, value_ref, taps_ref, cotangent_ref, send_ref):
    rows = 2 * chunks + 1
    for chunk in range(chunks):
        part = pl.ds(chunk * LANES, LANES)
        gate = key_ref[part, :].astype(jnp.float32) * value_ref[part, :].astype(jnp.float32)
        send_ref[pl.ds(chunk, LANES, stride=rows), :] = gate.T
        grad = query_ref[part, :].astype(jnp.float32) * cotangent_ref[part, :].astype(jnp.float32)
        send_ref[pl.ds(chunks + chunk, LANES, stride=rows), :] = grad.T
    place = place_ref[0]
    start = pl.multiple_of(lax.div(place, 2) * LANES, LANES)
    taps = taps_ref[pl.ds(start, LANES), :].T
    lane = lax.broadcasted_iota(jnp.int32, (LANES, LANES), 1)
    mine = lax.div(lane, LANES // 2) == lax.rem(place, 2)
    send_ref[pl.ds(2 * chunks, LANES, stride=rows), :] = jnp.where(mine, taps, 0.0)


def forward_kernel(
    blocks, chunks, recv_ref, first_ref, twist_ref, second_ref, inverse_ref, first_inv_ref, spec_ref, terms_ref, high_ref, low_ref
):
    rows = 2 * chunks + 1
    first = blocks * chunks
    columns = 2 * chunks
    stride = columns * rows
    cosine = twist_ref[:, :LANES]
    sine = twist_ref[:, LANES:]

    def read(column, signal):
        return jnp.concatenate(
            [recv_ref[pl.ds(column * rows + signal * chunks + chunk, blocks, stride=stride), :] for chunk in range(chunks)], 0
        )

    taps = jnp.concatenate(
        [
            recv_ref[pl.ds(2 * chunk * rows + rows - 1, blocks, stride=stride), :]
            + recv_ref[pl.ds((2 * chunk + 1) * rows + rows - 1, blocks, stride=stride), :]
            for chunk in range(chunks)
        ],
        0,
    )
    signals = [read(column, signal) for signal in range(2) for column in range(columns)] + [taps]
    for start in range(0, len(signals), 2):
        group = signals[start : start + 2]
        wide = jnp.concatenate(group, 1) if len(group) > 1 else group[0]
        high, low = split(wide)
        mixed = dot(first_ref[...], jnp.concatenate([high, low, high], 0))
        for offset in range(len(group)):
            lanes = slice(offset * LANES, (offset + 1) * LANES)
            real, imag = mixed[:first, lanes], mixed[first:, lanes]
            high, low = split(jnp.concatenate([real * cosine - imag * sine, imag * cosine + real * sine], 1))
            place = pl.ds((start + offset) * first, first)
            high_ref[place, :] = high
            low_ref[place, :] = low
    spec_ref[...] = second_stage(high_ref[...], low_ref[...], second_ref)
    real = jnp.zeros((first, LANES), jnp.float32)
    imag = jnp.zeros((first, LANES), jnp.float32)
    for column in range(columns):
        gate = pl.ds(column * first, first)
        grad = pl.ds((columns + column) * first, first)
        gate_real, gate_imag = spec_ref[gate, :LANES], spec_ref[gate, LANES:]
        grad_real, grad_imag = spec_ref[grad, :LANES], spec_ref[grad, LANES:]
        real = real + grad_real * gate_real + grad_imag * gate_imag
        imag = imag + grad_imag * gate_real - grad_real * gate_imag
    high, low = split(jnp.concatenate([real, imag], 1))
    back = second_stage(high, low, inverse_ref)
    real, imag = back[:, :LANES], back[:, LANES:]
    high, low = split(jnp.concatenate([real * cosine + imag * sine, imag * cosine - real * sine], 0))
    terms_ref[...] = dot(first_inv_ref[...], jnp.concatenate([high, low, high], 0))


def inverse_kernel(
    blocks, chunks, spec_ref, terms_ref, more_ref, twist_ref, inverse_ref, first_inv_ref, send_ref, high_ref, low_ref
):
    rows = 3 * chunks
    first = blocks * chunks
    columns = 2 * chunks
    stride = columns * rows
    cosine = twist_ref[:, :LANES]
    sine = twist_ref[:, LANES:]
    taps = pl.ds(2 * columns * first, first)
    taps_real, taps_imag = spec_ref[taps, :LANES], spec_ref[taps, LANES:]
    for column in range(columns):
        place = pl.ds(column * first, first)
        real, imag = spec_ref[place, :LANES], spec_ref[place, LANES:]
        high, low = split(jnp.concatenate([real * taps_real - imag * taps_imag, real * taps_imag + imag * taps_real], 1))
        high_ref[place, :] = high
        low_ref[place, :] = low
        place = pl.ds((columns + column) * first, first)
        real, imag = spec_ref[place, :LANES], spec_ref[place, LANES:]
        high, low = split(jnp.concatenate([real * taps_real + imag * taps_imag, imag * taps_real - real * taps_imag], 1))
        high_ref[place, :] = high
        low_ref[place, :] = low
    back = second_stage(high_ref[...], low_ref[...], inverse_ref)
    for signal in range(2):
        for column in range(0, columns, 2):
            sides = []
            for offset in range(2):
                begin = (signal * columns + column + offset) * first
                real, imag = back[begin : begin + first, :LANES], back[begin : begin + first, LANES:]
                sides.append(jnp.concatenate([real * cosine + imag * sine, imag * cosine - real * sine], 0))
            high, low = split(jnp.concatenate(sides, 1))
            result = dot(first_inv_ref[...], jnp.concatenate([high, low, high], 0))
            for offset in range(2):
                for chunk in range(chunks):
                    send_ref[pl.ds((column + offset) * rows + signal * chunks + chunk, blocks, stride=stride), :] = result[
                        chunk * blocks : (chunk + 1) * blocks, offset * LANES : (offset + 1) * LANES
                    ]
    total = terms_ref[...] + more_ref[...]
    for chunk in range(chunks):
        piece = total[chunk * blocks : (chunk + 1) * blocks, :]
        for column in range(columns):
            send_ref[pl.ds(column * rows + 2 * chunks + chunk, blocks, stride=stride), :] = piece


def output_kernel(
    chunks, scale, recv_ref, query_ref, key_ref, value_ref, cotangent_ref,
    gated_ref, grad_query_ref, grad_key_ref, grad_value_ref, grad_taps_ref,
):
    rows = 3 * chunks
    for chunk in range(chunks):
        part = pl.ds(chunk * LANES, LANES)
        conv = recv_ref[pl.ds(chunk, LANES, stride=rows), :].T
        gated_ref[part, :] = (query_ref[part, :].astype(jnp.float32) * conv).astype(jnp.bfloat16)
        grad_query_ref[part, :] = (cotangent_ref[part, :].astype(jnp.float32) * conv).astype(jnp.bfloat16)
        grad_gate = recv_ref[pl.ds(chunks + chunk, LANES, stride=rows), :].T
        grad_key_ref[part, :] = (grad_gate * value_ref[part, :].astype(jnp.float32)).astype(jnp.bfloat16)
        grad_value_ref[part, :] = (grad_gate * key_ref[part, :].astype(jnp.float32)).astype(jnp.bfloat16)
        grad_taps_ref[part, :] = recv_ref[pl.ds(2 * chunks + chunk, LANES, stride=rows), :].T * scale


def params():
    return pltpu.CompilerParams(vmem_limit_bytes=48 * 1024 * 1024)


def whole(count):
    return [pl.BlockSpec(memory_space=pltpu.VMEM)] * count


def pack(place, query, key, value, taps, cotangent):
    length = query.shape[0]
    chunks = length // LANES
    return pl.pallas_call(
        lambda *refs: pack_kernel(chunks, *refs),
        out_shape=jax.ShapeDtypeStruct((LANES * (2 * chunks + 1), LANES), jnp.float32),
        in_specs=[pl.BlockSpec(memory_space=pltpu.SMEM)] + whole(5),
        out_specs=whole(1)[0],
        compiler_params=params(),
        name="pack",
    )(place, query, key, value, taps, cotangent)


def forward(blocks, chunks, recv, first_fwd, twist, second_fwd, second_inv, first_inv):
    first = blocks * chunks
    count = (4 * chunks + 1) * first
    return pl.pallas_call(
        lambda *refs: forward_kernel(blocks, chunks, *refs),
        out_shape=(
            jax.ShapeDtypeStruct((count, 2 * LANES), jnp.float32),
            jax.ShapeDtypeStruct((first, LANES), jnp.float32),
        ),
        in_specs=whole(6),
        out_specs=tuple(whole(2)),
        scratch_shapes=[pltpu.VMEM((count, 2 * LANES), jnp.bfloat16)] * 2,
        compiler_params=params(),
        name="forward",
    )(recv, first_fwd, twist, second_fwd, second_inv, first_inv)


def inverse(blocks, chunks, spec, terms, more, twist, second_inv, first_inv):
    count = 4 * chunks * blocks * chunks
    return pl.pallas_call(
        lambda *refs: inverse_kernel(blocks, chunks, *refs),
        out_shape=jax.ShapeDtypeStruct((LANES * 3 * chunks, LANES), jnp.float32),
        in_specs=whole(6),
        out_specs=whole(1)[0],
        scratch_shapes=[pltpu.VMEM((count, 2 * LANES), jnp.bfloat16)] * 2,
        compiler_params=params(),
        name="inverse",
    )(spec, terms, more, twist, second_inv, first_inv)


def outputs(scale, recv, query, key, value, cotangent):
    length = query.shape[0]
    chunks = length // LANES
    rows = jax.ShapeDtypeStruct((length, LANES), jnp.bfloat16)
    return pl.pallas_call(
        lambda *refs: output_kernel(chunks, scale, *refs),
        out_shape=(rows, rows, rows, rows, jax.ShapeDtypeStruct((length, LANES), jnp.float32)),
        in_specs=whole(5),
        out_specs=tuple(whole(5)),
        compiler_params=params(),
        name="outputs",
    )(recv, query, key, value, cotangent)


def exchange(rows):
    shape = rows.shape
    flat = rows.reshape(LANES, 1, -1)
    return lax.all_to_all(flat, GROUP, 0, 0, tiled=True).reshape(shape)


def on_device(query, key, value, taps, cotangent):
    blocks = lax.axis_size("ctx")
    length = query.shape[0]
    chunks = length // LANES
    first_fwd, twist, second_fwd, second_inv, first_inv = (
        jnp.asarray(table) for table in dft_tables(blocks, chunks)
    )
    place = lax.axis_index(("y", "core")).astype(jnp.int32).reshape(1)
    recv = exchange(pack(place, query, key, value, taps, cotangent))
    spec, terms = forward(blocks, chunks, recv, first_fwd, twist, second_fwd, second_inv, first_inv)
    terms = terms + lax.ppermute(terms, "zh", PAIRS_NEAR)
    more = lax.ppermute(terms, "zh", PAIRS_ROUND)
    back = exchange(inverse(blocks, chunks, spec, terms, more, twist, second_inv, first_inv))
    scale = 1.0 / math.sqrt(float(blocks * length * lax.axis_size(("y", "zh", "core"))))
    return outputs(scale, back, query, key, value, cotangent)


def solution(mesh):
    split_mesh = Mesh(mesh.devices.reshape(mesh.shape["ctx"], 4, 4, 2), ("ctx", "y", "zh", "core"))
    tp = ("y", "zh", "core")
    wide = P("ctx", tp)
    return jax.shard_map(
        on_device,
        mesh=split_mesh,
        in_specs=(wide, wide, wide, P("ctx", None), wide),
        out_specs=(wide, wide, wide, wide, P("ctx", None)),
        check_vma=False,
    )
```

time: 646 us -> 95.3 us (0.15); the launches traced: 638 us -> 95 us
  waiting for transfers between devices: 489 us -> 6.69 us
  blocking collectives: 0 us -> 64.5 us
  starting transfers between devices: 78.9 us -> 14.5 us
  matrix products: 32.4 us -> 0 us
  local copies, waits for them, and re-layouts: 18.9 us -> 4.61 us
  between operations: 14.7 us -> 0.76 us
    psum x1 -> x0, waiting for transfers between devices: 344 us -> none  [on_device(): summed = lax.psum(filter_terms, 'tp')]
    all_to_all x12 -> x0, waiting for transfers between devices: 145 us -> none  [the longest x2 32.7 us: spread_inverse(): lax.all_to_all(part_real, 'ctx', split_axis=2, concat_axis=1, tiled=True)]
    all_to_all x12 -> x0, starting transfers between devices: 78.9 us -> none  [the longest x2 13.9 us: spread_forward(): lax.all_to_all(part_imag, 'ctx', split_axis=1, concat_axis=2, tiled=True)]
    all_to_all x0 -> x2, blocking collectives: none -> 64.5 us  [exchange(): return lax.all_to_all(flat, GROUP, 0, 0, tiled=True).reshape(shape)]
    dot_general x24 -> x0, matrix products: 32.4 us -> none  [the longest x2 4.02 us: spread_forward(): jnp.einsum('kn,gjnc->gjkc', cosine_second, part_real, precision=PRECISE)]
    ppermute x0 -> x2, starting transfers between devices: none -> 14.5 us  [the longest x1 8.81 us: on_device(): terms = terms + lax.ppermute(terms, 'zh', PAIRS_NEAR)]
    ppermute x0 -> x2, waiting for transfers between devices: none -> 6.69 us  [the longest x1 3.83 us: on_device(): terms = terms + lax.ppermute(terms, 'zh', PAIRS_NEAR)]
  transfers between devices with their start and end apart: 13 -> 2, of which waited for: 13 -> 2; matrix products, arithmetic and copies ran while one was open for 6% -> 0% of each run, Pallas kernels for 0% -> 0%
where the time goes in v1:
time: 95.3 us; the launch traced here: 95 us
  blocking collectives  64.5 us (68%)
  starting transfers between devices  14.5 us (15%)
  waiting for transfers between devices  6.69 us (7%)
  local copies, waits for them, and re-layouts  4.61 us (5%)
  Pallas kernels  3.94 us (4%)
    all_to_all x2, blocking collectives, exchange(): return lax.all_to_all(flat, GROUP, 0, 0, tiled=True).reshape(shape)  64.5 us
    ppermute x1, starting transfers between devices, on_device(): terms = terms + lax.ppermute(terms, 'zh', PAIRS_NEAR)  8.81 us
    ppermute x1, starting transfers between devices, on_device(): more = lax.ppermute(terms, 'zh', PAIRS_ROUND)  5.68 us
    unnamed x28, local copies, waits for them, and re-layouts  4.61 us
    ppermute x1, waiting for transfers between devices, on_device(): terms = terms + lax.ppermute(terms, 'zh', PAIRS_NEAR)  3.83 us
    ppermute x1, waiting for transfers between devices, on_device(): more = lax.ppermute(terms, 'zh', PAIRS_ROUND)  2.87 us
  transfers between devices with their start and end apart: 2, of which 2 were waited for; matrix products, arithmetic and copies ran while one was open for 0% of the time, Pallas kernels for 0%

profile of v1, /device:TPU:1, one launch (start us, length us, event | category | flops | bytes accessed | tf_op | source)
XLA Modules:
  0.0 95.0 jit_solution(4138910836176728054)
XLA Ops:
  0.6 0.0 copy-start.1
  0.6 0.9 copy-done.1
  1.5 0.0 copy-start.3
  1.5 0.9 copy-done.3
  2.4 0.0 copy-start.5
  2.5 0.9 copy-done.5
  3.4 0.0 copy-start.7
  3.4 0.9 copy-done.7
  4.3 0.0 copy-start.9
  4.3 0.9 copy-done.9
  5.2 0.0 copy-start
  5.2 0.0 copy-start.10
  5.2 0.0 copy-start.11
  5.2 0.0 copy-start.12
  5.2 0.0 copy-start.13
  5.2 0.2 pack.1
  5.5 33.4 %all_to_all.10 = f32[128,1,1152]{2,1,0:T(1,128)S(1)} all-to-all(f32[128,1,1152]{2,1,0:T(1,128)S(1)} %bitcast.7), channel_id=1, replica_groups=mesh['ctx'=16,'y'=4,'zh'=4,'core'=2] {'ctx','y','core'}, dimensions={0} | all-to-all | bytes 1179648 | tf_op jit(solution)/shard_map/all_to_all | solution.py:258
  38.8 0.0 copy-done
  38.8 0.0 copy-done.10
  38.8 0.0 copy-done.11
  38.9 0.0 copy-done.12
  38.9 0.0 copy-done.13
  38.9 1.2 %forward.1 = (f32[1088,256]{1,0:T(8,128)S(1)}, f32[64,128]{1,0:T(8,128)S(1)}) custom-call(f32[1152,128]{1,0:T(8,128)S(1)} %bitcast.8, bf16[128,192]{1,0:T(8,128)(2,1)S(1)} %copy-done.13, f32[64,256]{1,0:T(8,128)S(1)} %copy-done.11, bf16[512,256]{1,0:T(8,128)(2,1)S(1)} %copy-done.10, bf16[512,256]{1,0:T(8,128)(2,1)S(1)} %copy-done, bf16[64,384]{1,0:T(8,128)(2,1)S(1)} %copy-done.12), custom_call_target="tpu_custom_call" | custom-call | tf_op jit(solution)/shard_map/forward/pallas_call | solution.py:214
  40.1 8.8 %collective-permute-start = (f32[64,128]{1,0:T(8,128)S(1)}, f32[64,128]{1,0:T(8,128)S(1)}, u32[]{:S(2)}, u32[]{:S(2)}) collective-permute-start(f32[64,128]{1,0:T(8,128)S(1)} %get-tuple-element.8), channel_id=1, source_target_pairs={{0,2},{2,0},{4,6},{6,4},{1,3},{3,1},{5,7},{7,5},{8,10},{10,8},{12,... | collective-permute-start | bytes 98312 | tf_op jit(solution)/shard_map/ppermute | solution.py:271
  48.9 3.8 %collective-permute-done = f32[64,128]{1,0:T(8,128)S(1)} collective-permute-done((f32[64,128]{1,0:T(8,128)S(1)}, f32[64,128]{1,0:T(8,128)S(1)}, u32[]{:S(2)}, u32[]{:S(2)}) %collective-permute-start) | collective-permute-done | bytes 32800 | tf_op jit(solution)/shard_map/ppermute | solution.py:271
  52.8 5.7 %collective-permute-start.1 = (f32[64,128]{1,0:T(8,128)S(1)}, f32[64,128]{1,0:T(8,128)S(1)}, u32[]{:S(2)}, u32[]{:S(2)}) collective-permute-start(f32[64,128]{1,0:T(8,128)S(1)} %add.7.refs_1_), channel_id=1, source_target_pairs={{0,6},{6,0},{2,4},{4,2},{1,7},{7,1},{3,5},{5,3},{8,14},{14,8},{10,... | collective-permute-start | bytes 98312 | tf_op jit(solution)/shard_map/ppermute | solution.py:272
  58.4 2.9 %collective-permute-done.1.refs_2_ = f32[64,128]{1,0:T(8,128)S(1)} collective-permute-done((f32[64,128]{1,0:T(8,128)S(1)}, f32[64,128]{1,0:T(8,128)S(1)}, u32[]{:S(2)}, u32[]{:S(2)}) %collective-permute-start.1) | collective-permute-done | bytes 32800 | tf_op jit(solution)/shard_map/ppermute | solution.py:272
  61.3 1.4 %inverse.1 = f32[1536,128]{1,0:T(8,128)S(1)} custom-call(f32[1088,256]{1,0:T(8,128)S(1)} %get-tuple-element.7.refs_0_, f32[64,128]{1,0:T(8,128)S(1)} %add.7.refs_1_, f32[64,128]{1,0:T(8,128)S(1)} %collective-permute-done.1.refs_2_, f32[64,256]{1,0:T(8,128)S(1)} %copy-done.11, bf16[512,256]{1,0:T(8,128)(2,1)S(1)} %copy-done, bf16[64,384]{1,0:T(8,128)(2,1)S(1)} %copy-done.12), custom_call_target="tpu_custom_call" | custom-call | tf_op jit(solution)/shard_map/inverse/pallas_call | solution.py:230
  62.7 0.0 copy-start.2
  62.7 0.0 copy-start.4
  62.7 0.0 copy-start.6
  62.7 0.0 copy-start.8
  62.7 31.1 %all_to_all.11 = f32[128,1,1536]{2,1,0:T(1,128)S(1)} all-to-all(f32[128,1,1536]{2,1,0:T(1,128)S(1)} %bitcast.6), channel_id=1, replica_groups=mesh['ctx'=16,'y'=4,'zh'=4,'core'=2] {'ctx','y','core'}, dimensions={0} | all-to-all | bytes 1572864 | tf_op jit(solution)/shard_map/all_to_all | solution.py:258
  93.8 0.0 copy-done.2
  93.8 0.0 copy-done.4
  93.8 0.0 copy-done.6
  93.8 0.0 copy-done.8
  93.9 1.1 %outputs.1 = (bf16[512,128]{1,0:T(8,128)(2,1)}, bf16[512,128]{1,0:T(8,128)(2,1)}, bf16[512,128]{1,0:T(8,128)(2,1)}, bf16[512,128]{1,0:T(8,128)(2,1)}, f32[512,128]{1,0:T(8,128)}) custom-call(f32[1536,128]{1,0:T(8,128)S(1)} %bitcast.5, bf16[512,128]{1,0:T(8,128)(2,1)S(1)} %copy-done.2, bf16[512,128]{1,0:T(8,128)(2,1)S(1)} %copy-done.4, ...), custom_call_target="tpu_custom_call" | custom-call | tf_op jit(solution)/shard_map/outputs/pallas_call | solution.py:245
  (1 shorter events, 0.0 us)
Async XLA Ops:
  0.6 0.9 copy-start.1
  1.5 0.9 copy-start.3
  2.4 0.9 copy-start.5
  3.4 0.9 copy-start.7
  4.3 0.9 %copy-start.9 = (f32[512,128]{1,0:T(8,128)S(1)}, f32[512,128]{1,0:T(8,128)}, u32[]{:S(2)}) copy-start(f32[512,128]{1,0:T(8,128)} %refs_4_.4) | copy-start | bytes 786436
  5.2 33.6 %copy-start = (bf16[512,256]{1,0:T(8,128)(2,1)S(1)}, bf16[512,256]{1,0:T(8,128)(2,1)}, u32[]{:S(2)}) copy-start(bf16[512,256]{1,0:T(8,128)(2,1)} %constant.24.clone.refs_4_) | copy-start | bytes 786436
  5.2 33.6 %copy-start.10 = (bf16[512,256]{1,0:T(8,128)(2,1)S(1)}, bf16[512,256]{1,0:T(8,128)(2,1)}, u32[]{:S(2)}) copy-start(bf16[512,256]{1,0:T(8,128)(2,1)} %constant.23.clone.refs_3_) | copy-start | bytes 786436
  5.2 33.6 %copy-start.11 = (f32[64,256]{1,0:T(8,128)S(1)}, f32[64,256]{1,0:T(8,128)}, u32[]{:S(2)}) copy-start(f32[64,256]{1,0:T(8,128)} %constant.22.clone.refs_2_.refs_3_) | copy-start | bytes 196612
  5.2 33.6 %copy-start.12 = (bf16[64,384]{1,0:T(8,128)(2,1)S(1)}, bf16[64,384]{1,0:T(8,128)(2,1)}, u32[]{:S(2)}) copy-start(bf16[64,384]{1,0:T(8,128)(2,1)} %constant.25.clone.refs_5_) | copy-start | bytes 147460
  5.2 33.6 %copy-start.13 = (bf16[128,192]{1,0:T(8,128)(2,1)S(1)}, bf16[128,192]{1,0:T(8,128)(2,1)}, u32[]{:S(2)}) copy-start(bf16[128,192]{1,0:T(8,128)(2,1)} %constant.21.clone.refs_1_) | copy-start | bytes 147460
  40.1 12.6 %collective-permute-start = (f32[64,128]{1,0:T(8,128)S(1)}, f32[64,128]{1,0:T(8,128)S(1)}, u32[]{:S(2)}, u32[]{:S(2)}) collective-permute-start(f32[64,128]{1,0:T(8,128)S(1)} %get-tuple-element.8), channel_id=1, source_target_pairs={{0,2},{2,0},{4,6},{6,4},{1,3},{3,1},{5,7},{7,5},{8,10},{10,8},{12,... | collective-permute-start | bytes 98312 | tf_op jit(solution)/shard_map/ppermute | solution.py:271
  52.8 8.6 %collective-permute-start.1 = (f32[64,128]{1,0:T(8,128)S(1)}, f32[64,128]{1,0:T(8,128)S(1)}, u32[]{:S(2)}, u32[]{:S(2)}) collective-permute-start(f32[64,128]{1,0:T(8,128)S(1)} %add.7.refs_1_), channel_id=1, source_target_pairs={{0,6},{6,0},{2,4},{4,2},{1,7},{7,1},{3,5},{5,3},{8,14},{14,8},{10,... | collective-permute-start | bytes 98312 | tf_op jit(solution)/shard_map/ppermute | solution.py:272
  62.7 31.1 %copy-start.2 = (bf16[512,128]{1,0:T(8,128)(2,1)S(1)}, bf16[512,128]{1,0:T(8,128)(2,1)}, u32[]{:S(2)}) copy-start(bf16[512,128]{1,0:T(8,128)(2,1)} %refs_1_.4) | copy-start | bytes 393220
  62.7 31.1 %copy-start.4 = (bf16[512,128]{1,0:T(8,128)(2,1)S(1)}, bf16[512,128]{1,0:T(8,128)(2,1)}, u32[]{:S(2)}) copy-start(bf16[512,128]{1,0:T(8,128)(2,1)} %refs_2_.4) | copy-start | bytes 393220
  62.7 31.1 %copy-start.6 = (bf16[512,128]{1,0:T(8,128)(2,1)S(1)}, bf16[512,128]{1,0:T(8,128)(2,1)}, u32[]{:S(2)}) copy-start(bf16[512,128]{1,0:T(8,128)(2,1)} %refs_3_.5) | copy-start | bytes 393220
  62.7 31.1 %copy-start.8 = (bf16[512,128]{1,0:T(8,128)(2,1)S(1)}, bf16[512,128]{1,0:T(8,128)(2,1)}, u32[]{:S(2)}) copy-start(bf16[512,128]{1,0:T(8,128)(2,1)} %refs_4_.5) | copy-start | bytes 393220

commit v2 on v1

--- a/solution.py
+++ b/solution.py
@@ -58,20 +58,39 @@
     return dot(high, table_high) + dot(low, table_high) + dot(high, table_low)
 
 
-def pack_kernel(chunks, place_ref, query_ref, key_ref, value_ref, taps_ref, cotangent_ref, send_ref):
+def pack_kernel(
+    chunks, place_ref, query_hbm, key_hbm, value_hbm, taps_hbm, cotangent_hbm, send_ref,
+    query_ref, key_ref, value_ref, taps_ref, cotangent_ref, done_ref,
+):
     rows = 2 * chunks + 1
+    place = place_ref[0]
+    start = pl.multiple_of(lax.div(place, 2) * LANES, LANES)
+    pairs = (
+        (key_hbm, key_ref),
+        (value_hbm, value_ref),
+        (query_hbm, query_ref),
+        (cotangent_hbm, cotangent_ref),
+        (taps_hbm.at[pl.ds(start, LANES), :], taps_ref),
+    )
+    copies = [pltpu.make_async_copy(source, target, done_ref.at[n]) for n, (source, target) in enumerate(pairs)]
+    for copy in copies:
+        copy.start()
+    copies[0].wait()
+    copies[1].wait()
     for chunk in range(chunks):
         part = pl.ds(chunk * LANES, LANES)
         gate = key_ref[part, :].astype(jnp.float32) * value_ref[part, :].astype(jnp.float32)
         send_ref[pl.ds(chunk, LANES, stride=rows), :] = gate.T
+    copies[2].wait()
+    copies[3].wait()
+    for chunk in range(chunks):
+        part = pl.ds(chunk * LANES, LANES)
         grad = query_ref[part, :].astype(jnp.float32) * cotangent_ref[part, :].astype(jnp.float32)
         send_ref[pl.ds(chunks + chunk, LANES, stride=rows), :] = grad.T
-    place = place_ref[0]
-    start = pl.multiple_of(lax.div(place, 2) * LANES, LANES)
-    taps = taps_ref[pl.ds(start, LANES), :].T
+    copies[4].wait()
     lane = lax.broadcasted_iota(jnp.int32, (LANES, LANES), 1)
     mine = lax.div(lane, LANES // 2) == lax.rem(place, 2)
-    send_ref[pl.ds(2 * chunks, LANES, stride=rows), :] = jnp.where(mine, taps, 0.0)
+    send_ref[pl.ds(2 * chunks, LANES, stride=rows), :] = jnp.where(mine, taps_ref[...].T, 0.0)
 
 
 def forward_kernel(
@@ -127,13 +146,9 @@
     terms_ref[...] = dot(first_inv_ref[...], jnp.concatenate([high, low, high], 0))
 
 
-def inverse_kernel(
-    blocks, chunks, spec_ref, terms_ref, more_ref, twist_ref, inverse_ref, first_inv_ref, send_ref, high_ref, low_ref
-):
-    rows = 3 * chunks
+def inverse_kernel(blocks, chunks, spec_ref, twist_ref, inverse_ref, first_inv_ref, send_ref, high_ref, low_ref):
     first = blocks * chunks
     columns = 2 * chunks
-    stride = columns * rows
     cosine = twist_ref[:, :LANES]
     sine = twist_ref[:, LANES:]
     taps = pl.ds(2 * columns * first, first)
@@ -149,6 +164,8 @@
         high, low = split(jnp.concatenate([real * taps_real + imag * taps_imag, imag * taps_real - real * taps_imag], 1))
         high_ref[place, :] = high
         low_ref[place, :] = low
+    rows = 3 * chunks
+    stride = columns * rows
     back = second_stage(high_ref[...], low_ref[...], inverse_ref)
     for signal in range(2):
         for column in range(0, columns, 2):
@@ -164,11 +181,19 @@
                     send_ref[pl.ds((column + offset) * rows + signal * chunks + chunk, blocks, stride=stride), :] = result[
                         chunk * blocks : (chunk + 1) * blocks, offset * LANES : (offset + 1) * LANES
                     ]
-    total = terms_ref[...] + more_ref[...]
+
+
+def fill_kernel(blocks, chunks, count, send_in_ref, *refs):
+    columns = 2 * chunks
+    rows = 3 * chunks
+    total = refs[0][...]
+    for ref in refs[1:count]:
+        total = total + ref[...]
+    send_ref = refs[count]
     for chunk in range(chunks):
         piece = total[chunk * blocks : (chunk + 1) * blocks, :]
         for column in range(columns):
-            send_ref[pl.ds(column * rows + 2 * chunks + chunk, blocks, stride=stride), :] = piece
+            send_ref[pl.ds(column * rows + 2 * chunks + chunk, blocks, stride=columns * rows), :] = piece
 
 
 def output_kernel(
@@ -198,14 +223,16 @@
 def pack(place, query, key, value, taps, cotangent):
     length = query.shape[0]
     chunks = length // LANES
+    wide = pltpu.VMEM((length, LANES), jnp.bfloat16)
     return pl.pallas_call(
         lambda *refs: pack_kernel(chunks, *refs),
         out_shape=jax.ShapeDtypeStruct((LANES * (2 * chunks + 1), LANES), jnp.float32),
-        in_specs=[pl.BlockSpec(memory_space=pltpu.SMEM)] + whole(5),
+        in_specs=[pl.BlockSpec(memory_space=pltpu.SMEM)] + [pl.BlockSpec(memory_space=pltpu.HBM)] * 5,
         out_specs=whole(1)[0],
+        scratch_shapes=[wide, wide, wide, pltpu.VMEM((LANES, LANES), jnp.float32), wide, pltpu.SemaphoreType.DMA((5,))],
         compiler_params=params(),
         name="pack",
-    )(place, query, key, value, taps, cotangent)
+    )(place, *(pltpu.with_memory_space_constraint(array, pltpu.HBM) for array in (query, key, value, taps, cotangent)))
 
 
 def forward(blocks, chunks, recv, first_fwd, twist, second_fwd, second_inv, first_inv):
@@ -225,17 +252,30 @@
     )(recv, first_fwd, twist, second_fwd, second_inv, first_inv)
 
 
-def inverse(blocks, chunks, spec, terms, more, twist, second_inv, first_inv):
+def inverse(blocks, chunks, spec, twist, second_inv, first_inv):
     count = 4 * chunks * blocks * chunks
     return pl.pallas_call(
         lambda *refs: inverse_kernel(blocks, chunks, *refs),
         out_shape=jax.ShapeDtypeStruct((LANES * 3 * chunks, LANES), jnp.float32),
-        in_specs=whole(6),
+        in_specs=whole(4),
         out_specs=whole(1)[0],
         scratch_shapes=[pltpu.VMEM((count, 2 * LANES), jnp.bfloat16)] * 2,
         compiler_params=params(),
+        cost_estimate=pl.CostEstimate(flops=10**9, bytes_accessed=4 * 10**6, transcendentals=0),
         name="inverse",
-    )(spec, terms, more, twist, second_inv, first_inv)
+    )(spec, twist, second_inv, first_inv)
+
+
+def fill(blocks, chunks, send, *terms):
+    return pl.pallas_call(
+        lambda *refs: fill_kernel(blocks, chunks, len(terms), *refs),
+        out_shape=jax.ShapeDtypeStruct(send.shape, jnp.float32),
+        in_specs=whole(1 + len(terms)),
+        out_specs=whole(1)[0],
+        input_output_aliases={0: 0},
+        compiler_params=params(),
+        name="fill",
+    )(send, *terms)
 
 
 def outputs(scale, recv, query, key, value, cotangent):
@@ -268,9 +308,10 @@
     place = lax.axis_index(("y", "core")).astype(jnp.int32).reshape(1)
     recv = exchange(pack(place, query, key, value, taps, cotangent))
     spec, terms = forward(blocks, chunks, recv, first_fwd, twist, second_fwd, second_inv, first_inv)
+    send = inverse(blocks, chunks, spec, twist, second_inv, first_inv)
     terms = terms + lax.ppermute(terms, "zh", PAIRS_NEAR)
-    more = lax.ppermute(terms, "zh", PAIRS_ROUND)
-    back = exchange(inverse(blocks, chunks, spec, terms, more, twist, second_inv, first_inv))
+    send = fill(blocks, chunks, send, terms, lax.ppermute(terms, "zh", PAIRS_ROUND))
+    back = exchange(send)
     scale = 1.0 / math.sqrt(float(blocks * length * lax.axis_size(("y", "zh", "core"))))
     return outputs(scale, back, query, key, value, cotangent)
 

time: 95.3 us -> 90.7 us (0.952)
  local copies, waits for them, and re-layouts: 4.61 us -> 0.06 us
  waiting for transfers between devices: 6.69 us -> 5.49 us
  Pallas kernels: 3.94 us -> 5.13 us
    unnamed x28 -> x18, local copies, waits for them, and re-layouts: 4.61 us -> 0.06 us
    pallas_call x1, Pallas kernels: 0.24 us -> 1.45 us  [pack(): pl.pallas_call(lambda *refs: pack_kernel(chunks, *refs), out_shape=jax.Sh...]
    ppermute x1, waiting for transfers between devices: 2.87 us -> 1.66 us  [on_device(): lax.ppermute(terms, 'zh', PAIRS_ROUND)]
  transfers between devices with their start and end apart: 2 -> 2, of which waited for: 2 -> 2; matrix products, arithmetic and copies ran while one was open for 0% -> 0% of each run, Pallas kernels for 0% -> 1%
where the time goes in v2:
time: 90.7 us; the launch traced here: 90.4 us
  blocking collectives  64.4 us (71%)
  starting transfers between devices  14.5 us (16%)
  waiting for transfers between devices  5.49 us (6%)
  Pallas kernels  5.13 us (6%)
    all_to_all x2, blocking collectives, exchange(): return lax.all_to_all(flat, GROUP, 0, 0, tiled=True).reshape(shape)  64.4 us
    ppermute x1, starting transfers between devices, on_device(): terms = terms + lax.ppermute(terms, 'zh', PAIRS_NEAR)  8.82 us
    ppermute x1, starting transfers between devices, on_device(): lax.ppermute(terms, 'zh', PAIRS_ROUND)  5.67 us
    ppermute x1, waiting for transfers between devices, on_device(): terms = terms + lax.ppermute(terms, 'zh', PAIRS_NEAR)  3.84 us
  transfers between devices with their start and end apart: 2, of which 2 were waited for; matrix products, arithmetic and copies ran while one was open for 0% of the time, Pallas kernels for 1%

profile of v2, /device:TPU:1, one launch (start us, length us, event | category | flops | bytes accessed | tf_op | source)
XLA Modules:
  0.0 90.4 jit_solution(13361906735911048636)
XLA Ops:
  0.6 0.0 copy-start.4
  0.6 0.0 copy-start.5
  0.7 0.0 copy-start.6
  0.7 0.0 copy-start.7
  0.7 0.0 copy-start.8
  0.7 1.4 %pack.1 = f32[1152,128]{1,0:T(8,128)S(1)} custom-call(s32[1]{0:T(128)} %bitcast.refs_0_, bf16[512,128]{1,0:T(8,128)(2,1)} %refs_1_.5, bf16[512,128]{1,0:T(8,128)(2,1)} %refs_2_.5, bf16[512,128]{1,0:T(8,128)(2,1)} %refs_3_.5, f32[512,128]{1,0:T(8,128)} %refs_4_.3, bf16[512,128]{1,0:T(8,128)(2,1)} %refs_4_.4), custom_call_target="tpu_custom_call" | custom-call | tf_op jit(solution)/shard_map/pack/pallas_call | solution.py:227
  2.2 33.4 %all_to_all.10 = f32[128,1,1152]{2,1,0:T(1,128)S(1)} all-to-all(f32[128,1,1152]{2,1,0:T(1,128)S(1)} %bitcast.7), channel_id=1, replica_groups=mesh['ctx'=16,'y'=4,'zh'=4,'core'=2] {'ctx','y','core'}, dimensions={0} | all-to-all | bytes 1179648 | tf_op jit(solution)/shard_map/all_to_all | solution.py:298
  35.5 0.0 copy-done.4
  35.5 0.0 copy-done.5
  35.5 0.0 copy-done.6
  35.5 0.0 copy-done.7
  35.5 0.0 copy-done.8
  35.6 1.2 %forward.1 = (f32[1088,256]{1,0:T(8,128)S(1)}, f32[64,128]{1,0:T(8,128)S(1)}) custom-call(f32[1152,128]{1,0:T(8,128)S(1)} %bitcast.8, bf16[128,192]{1,0:T(8,128)(2,1)S(1)} %copy-done.7, f32[64,256]{1,0:T(8,128)S(1)} %copy-done.6, bf16[512,256]{1,0:T(8,128)(2,1)S(1)} %copy-done.5, bf16[512,256]{1,0:T(8,128)(2,1)S(1)} %copy-done.4, bf16[64,384]{1,0:T(8,128)(2,1)S(1)} %copy-done.8), custom_call_target="tpu_custom_call" | custom-call | tf_op jit(solution)/shard_map/forward/pallas_call | solution.py:241
  36.8 8.8 %collective-permute-start = (f32[64,128]{1,0:T(8,128)S(1)}, f32[64,128]{1,0:T(8,128)S(1)}, u32[]{:S(2)}, u32[]{:S(2)}) collective-permute-start(f32[64,128]{1,0:T(8,128)S(1)} %get-tuple-element.8), channel_id=1, source_target_pairs={{0,2},{2,0},{4,6},{6,4},{1,3},{3,1},{5,7},{7,5},{8,10},{10,8},{12,... | collective-permute-start | bytes 98312 | tf_op jit(solution)/shard_map/ppermute | solution.py:312
  45.6 3.8 %collective-permute-done = f32[64,128]{1,0:T(8,128)S(1)} collective-permute-done((f32[64,128]{1,0:T(8,128)S(1)}, f32[64,128]{1,0:T(8,128)S(1)}, u32[]{:S(2)}, u32[]{:S(2)}) %collective-permute-start) | collective-permute-done | bytes 32800 | tf_op jit(solution)/shard_map/ppermute | solution.py:312
  49.4 5.7 %collective-permute-start.1 = (f32[64,128]{1,0:T(8,128)S(1)}, f32[64,128]{1,0:T(8,128)S(1)}, u32[]{:S(2)}, u32[]{:S(2)}) collective-permute-start(f32[64,128]{1,0:T(8,128)S(1)} %add.7.refs_1_), channel_id=1, source_target_pairs={{0,6},{6,0},{2,4},{4,2},{1,7},{7,1},{3,5},{5,3},{8,14},{14,8},{10,... | collective-permute-start | bytes 98312 | tf_op jit(solution)/shard_map/ppermute | solution.py:313
  55.1 1.2 %inverse.1.refs_0_ = f32[1536,128]{1,0:T(8,128)S(1)} custom-call(f32[1088,256]{1,0:T(8,128)S(1)} %get-tuple-element.7.refs_0_, f32[64,256]{1,0:T(8,128)S(1)} %copy-done.6, bf16[512,256]{1,0:T(8,128)(2,1)S(1)} %copy-done.4, bf16[64,384]{1,0:T(8,128)(2,1)S(1)} %copy-done.8), custom_call_target="tpu_custom_call" | custom-call | flops 1000000000 | bytes 4000000 | tf_op jit(solution)/shard_map/inverse/pallas_call | solution.py:257
  56.3 1.7 %collective-permute-done.1.refs_2_ = f32[64,128]{1,0:T(8,128)S(1)} collective-permute-done((f32[64,128]{1,0:T(8,128)S(1)}, f32[64,128]{1,0:T(8,128)S(1)}, u32[]{:S(2)}, u32[]{:S(2)}) %collective-permute-start.1) | collective-permute-done | bytes 32800 | tf_op jit(solution)/shard_map/ppermute | solution.py:313
  58.0 0.1 fill.1
  58.1 0.0 copy-start
  58.2 0.0 copy-start.1
  58.2 0.0 copy-start.2
  58.2 0.0 copy-start.3
  58.2 31.1 %all_to_all.11 = f32[128,1,1536]{2,1,0:T(1,128)S(1)} all-to-all(f32[128,1,1536]{2,1,0:T(1,128)S(1)} %bitcast.5), channel_id=1, replica_groups=mesh['ctx'=16,'y'=4,'zh'=4,'core'=2] {'ctx','y','core'}, dimensions={0} | all-to-all | bytes 1572864 | tf_op jit(solution)/shard_map/all_to_all | solution.py:298
  89.3 0.0 copy-done
  89.3 0.0 copy-done.1
  89.3 0.0 copy-done.2
  89.3 0.0 copy-done.3
  89.3 1.1 %outputs.1 = (bf16[512,128]{1,0:T(8,128)(2,1)}, bf16[512,128]{1,0:T(8,128)(2,1)}, bf16[512,128]{1,0:T(8,128)(2,1)}, bf16[512,128]{1,0:T(8,128)(2,1)}, f32[512,128]{1,0:T(8,128)}) custom-call(f32[1536,128]{1,0:T(8,128)S(1)} %bitcast.6, bf16[512,128]{1,0:T(8,128)(2,1)S(1)} %copy-done, bf16[512,128]{1,0:T(8,128)(2,1)S(1)} %copy-done.1, ...), custom_call_target="tpu_custom_call" | custom-call | tf_op jit(solution)/shard_map/outputs/pallas_call | solution.py:285
  (1 shorter events, 0.0 us)
Async XLA Ops:
  0.6 34.9 %copy-start.4 = (bf16[512,256]{1,0:T(8,128)(2,1)S(1)}, bf16[512,256]{1,0:T(8,128)(2,1)}, u32[]{:S(2)}) copy-start(bf16[512,256]{1,0:T(8,128)(2,1)} %constant.24.clone.refs_4_.refs_2_) | copy-start | bytes 786436
  0.6 34.9 %copy-start.5 = (bf16[512,256]{1,0:T(8,128)(2,1)S(1)}, bf16[512,256]{1,0:T(8,128)(2,1)}, u32[]{:S(2)}) copy-start(bf16[512,256]{1,0:T(8,128)(2,1)} %constant.23.clone.refs_3_) | copy-start | bytes 786436
  0.7 34.9 %copy-start.6 = (f32[64,256]{1,0:T(8,128)S(1)}, f32[64,256]{1,0:T(8,128)}, u32[]{:S(2)}) copy-start(f32[64,256]{1,0:T(8,128)} %constant.22.clone.refs_2_.refs_1_) | copy-start | bytes 196612
  0.7 34.9 %copy-start.7 = (bf16[128,192]{1,0:T(8,128)(2,1)S(1)}, bf16[128,192]{1,0:T(8,128)(2,1)}, u32[]{:S(2)}) copy-start(bf16[128,192]{1,0:T(8,128)(2,1)} %constant.21.clone.refs_1_) | copy-start | bytes 147460
  0.7 34.9 %copy-start.8 = (bf16[64,384]{1,0:T(8,128)(2,1)S(1)}, bf16[64,384]{1,0:T(8,128)(2,1)}, u32[]{:S(2)}) copy-start(bf16[64,384]{1,0:T(8,128)(2,1)} %constant.25.clone.refs_5_.refs_3_) | copy-start | bytes 147460
  36.8 12.7 %collective-permute-start = (f32[64,128]{1,0:T(8,128)S(1)}, f32[64,128]{1,0:T(8,128)S(1)}, u32[]{:S(2)}, u32[]{:S(2)}) collective-permute-start(f32[64,128]{1,0:T(8,128)S(1)} %get-tuple-element.8), channel_id=1, source_target_pairs={{0,2},{2,0},{4,6},{6,4},{1,3},{3,1},{5,7},{7,5},{8,10},{10,8},{12,... | collective-permute-start | bytes 98312 | tf_op jit(solution)/shard_map/ppermute | solution.py:312
  49.4 8.6 %collective-permute-start.1 = (f32[64,128]{1,0:T(8,128)S(1)}, f32[64,128]{1,0:T(8,128)S(1)}, u32[]{:S(2)}, u32[]{:S(2)}) collective-permute-start(f32[64,128]{1,0:T(8,128)S(1)} %add.7.refs_1_), channel_id=1, source_target_pairs={{0,6},{6,0},{2,4},{4,2},{1,7},{7,1},{3,5},{5,3},{8,14},{14,8},{10,... | collective-permute-start | bytes 98312 | tf_op jit(solution)/shard_map/ppermute | solution.py:313
  58.1 31.1 %copy-start = (bf16[512,128]{1,0:T(8,128)(2,1)S(1)}, bf16[512,128]{1,0:T(8,128)(2,1)}, u32[]{:S(2)}) copy-start(bf16[512,128]{1,0:T(8,128)(2,1)} %refs_1_.5) | copy-start | bytes 393220
  58.2 31.1 %copy-start.1 = (bf16[512,128]{1,0:T(8,128)(2,1)S(1)}, bf16[512,128]{1,0:T(8,128)(2,1)}, u32[]{:S(2)}) copy-start(bf16[512,128]{1,0:T(8,128)(2,1)} %refs_2_.5) | copy-start | bytes 393220
  58.2 31.1 %copy-start.2 = (bf16[512,128]{1,0:T(8,128)(2,1)S(1)}, bf16[512,128]{1,0:T(8,128)(2,1)}, u32[]{:S(2)}) copy-start(bf16[512,128]{1,0:T(8,128)(2,1)} %refs_3_.5) | copy-start | bytes 393220
  58.2 31.1 %copy-start.3 = (bf16[512,128]{1,0:T(8,128)(2,1)S(1)}, bf16[512,128]{1,0:T(8,128)(2,1)}, u32[]{:S(2)}) copy-start(bf16[512,128]{1,0:T(8,128)(2,1)} %refs_4_.4) | copy-start | bytes 393220

commit v3 on v2

--- a/solution.py
+++ b/solution.py
@@ -164,7 +164,7 @@
         high, low = split(jnp.concatenate([real * taps_real + imag * taps_imag, imag * taps_real - real * taps_imag], 1))
         high_ref[place, :] = high
         low_ref[place, :] = low
-    rows = 3 * chunks
+    rows = 2 * chunks
     stride = columns * rows
     back = second_stage(high_ref[...], low_ref[...], inverse_ref)
     for signal in range(2):
@@ -183,13 +183,15 @@
                     ]
 
 
-def fill_kernel(blocks, chunks, count, send_in_ref, *refs):
+def fill_kernel(blocks, chunks, count, conv_ref, *refs):
     columns = 2 * chunks
     rows = 3 * chunks
     total = refs[0][...]
     for ref in refs[1:count]:
         total = total + ref[...]
     send_ref = refs[count]
+    for place in range(blocks * columns):
+        send_ref[pl.ds(place * rows, 2 * chunks), :] = conv_ref[pl.ds(place * 2 * chunks, 2 * chunks), :]
     for chunk in range(chunks):
         piece = total[chunk * blocks : (chunk + 1) * blocks, :]
         for column in range(columns):
@@ -256,7 +258,7 @@
     count = 4 * chunks * blocks * chunks
     return pl.pallas_call(
         lambda *refs: inverse_kernel(blocks, chunks, *refs),
-        out_shape=jax.ShapeDtypeStruct((LANES * 3 * chunks, LANES), jnp.float32),
+        out_shape=jax.ShapeDtypeStruct((LANES * 2 * chunks, LANES), jnp.float32),
         in_specs=whole(4),
         out_specs=whole(1)[0],
         scratch_shapes=[pltpu.VMEM((count, 2 * LANES), jnp.bfloat16)] * 2,
@@ -269,10 +271,9 @@
 def fill(blocks, chunks, send, *terms):
     return pl.pallas_call(
         lambda *refs: fill_kernel(blocks, chunks, len(terms), *refs),
-        out_shape=jax.ShapeDtypeStruct(send.shape, jnp.float32),
+        out_shape=jax.ShapeDtypeStruct((LANES * 3 * chunks, LANES), jnp.float32),
         in_specs=whole(1 + len(terms)),
         out_specs=whole(1)[0],
-        input_output_aliases={0: 0},
         compiler_params=params(),
         name="fill",
     )(send, *terms)

time: 90.7 us -> 90.7 us (level)
  no operation moved by 1% of the time
where the time goes in v3:
time: 90.7 us; the launch traced here: 90.5 us
  blocking collectives  64.4 us (71%)
  starting transfers between devices  14.5 us (16%)
  waiting for transfers between devices  5.49 us (6%)
  Pallas kernels  5.19 us (6%)
    all_to_all x2, blocking collectives, exchange(): return lax.all_to_all(flat, GROUP, 0, 0, tiled=True).reshape(shape)  64.4 us
    ppermute x1, starting transfers between devices, on_device(): terms = terms + lax.ppermute(terms, 'zh', PAIRS_NEAR)  8.82 us
    ppermute x1, starting transfers between devices, on_device(): lax.ppermute(terms, 'zh', PAIRS_ROUND)  5.67 us
    ppermute x1, waiting for transfers between devices, on_device(): terms = terms + lax.ppermute(terms, 'zh', PAIRS_NEAR)  3.84 us
  transfers between devices with their start and end apart: 2, of which 2 were waited for; matrix products, arithmetic and copies ran while one was open for 0% of the time, Pallas kernels for 1%

profile of v3, /device:TPU:1, one launch (start us, length us, event | category | flops | bytes accessed | tf_op | source)
XLA Modules:
  0.0 90.5 jit_solution(2257848570507260231)
XLA Ops:
  0.6 0.0 copy-start.4
  0.6 0.0 copy-start.5
  0.7 0.0 copy-start.6
  0.7 0.0 copy-start.7
  0.7 0.0 copy-start.8
  0.7 1.4 %pack.1 = f32[1152,128]{1,0:T(8,128)S(1)} custom-call(s32[1]{0:T(128)} %bitcast.refs_0_, bf16[512,128]{1,0:T(8,128)(2,1)} %refs_1_.5, bf16[512,128]{1,0:T(8,128)(2,1)} %refs_2_.5, bf16[512,128]{1,0:T(8,128)(2,1)} %refs_3_.5, f32[512,128]{1,0:T(8,128)} %refs_4_.3, bf16[512,128]{1,0:T(8,128)(2,1)} %refs_4_.4), custom_call_target="tpu_custom_call" | custom-call | tf_op jit(solution)/shard_map/pack/pallas_call | solution.py:229
  2.2 33.4 %all_to_all.10 = f32[128,1,1152]{2,1,0:T(1,128)S(1)} all-to-all(f32[128,1,1152]{2,1,0:T(1,128)S(1)} %bitcast.7), channel_id=1, replica_groups=mesh['ctx'=16,'y'=4,'zh'=4,'core'=2] {'ctx','y','core'}, dimensions={0} | all-to-all | bytes 1179648 | tf_op jit(solution)/shard_map/all_to_all | solution.py:299
  35.5 0.0 copy-done.4
  35.5 0.0 copy-done.5
  35.5 0.0 copy-done.6
  35.5 0.0 copy-done.7
  35.5 0.0 copy-done.8
  35.6 1.2 %forward.1 = (f32[1088,256]{1,0:T(8,128)S(1)}, f32[64,128]{1,0:T(8,128)S(1)}) custom-call(f32[1152,128]{1,0:T(8,128)S(1)} %bitcast.8, bf16[128,192]{1,0:T(8,128)(2,1)S(1)} %copy-done.7, f32[64,256]{1,0:T(8,128)S(1)} %copy-done.6, bf16[512,256]{1,0:T(8,128)(2,1)S(1)} %copy-done.5, bf16[512,256]{1,0:T(8,128)(2,1)S(1)} %copy-done.4, bf16[64,384]{1,0:T(8,128)(2,1)S(1)} %copy-done.8), custom_call_target="tpu_custom_call" | custom-call | tf_op jit(solution)/shard_map/forward/pallas_call | solution.py:243
  36.8 8.8 %collective-permute-start = (f32[64,128]{1,0:T(8,128)S(1)}, f32[64,128]{1,0:T(8,128)S(1)}, u32[]{:S(2)}, u32[]{:S(2)}) collective-permute-start(f32[64,128]{1,0:T(8,128)S(1)} %get-tuple-element.8), channel_id=1, source_target_pairs={{0,2},{2,0},{4,6},{6,4},{1,3},{3,1},{5,7},{7,5},{8,10},{10,8},{12,... | collective-permute-start | bytes 98312 | tf_op jit(solution)/shard_map/ppermute | solution.py:313
  45.6 3.8 %collective-permute-done = f32[64,128]{1,0:T(8,128)S(1)} collective-permute-done((f32[64,128]{1,0:T(8,128)S(1)}, f32[64,128]{1,0:T(8,128)S(1)}, u32[]{:S(2)}, u32[]{:S(2)}) %collective-permute-start) | collective-permute-done | bytes 32800 | tf_op jit(solution)/shard_map/ppermute | solution.py:313
  49.4 5.7 %collective-permute-start.1 = (f32[64,128]{1,0:T(8,128)S(1)}, f32[64,128]{1,0:T(8,128)S(1)}, u32[]{:S(2)}, u32[]{:S(2)}) collective-permute-start(f32[64,128]{1,0:T(8,128)S(1)} %add.7.refs_1_), channel_id=1, source_target_pairs={{0,6},{6,0},{2,4},{4,2},{1,7},{7,1},{3,5},{5,3},{8,14},{14,8},{10,... | collective-permute-start | bytes 98312 | tf_op jit(solution)/shard_map/ppermute | solution.py:314
  55.1 1.2 %inverse.1.refs_0_ = f32[1024,128]{1,0:T(8,128)S(1)} custom-call(f32[1088,256]{1,0:T(8,128)S(1)} %get-tuple-element.7.refs_0_, f32[64,256]{1,0:T(8,128)S(1)} %copy-done.6, bf16[512,256]{1,0:T(8,128)(2,1)S(1)} %copy-done.4, bf16[64,384]{1,0:T(8,128)(2,1)S(1)} %copy-done.8), custom_call_target="tpu_custom_call" | custom-call | flops 1000000000 | bytes 4000000 | tf_op jit(solution)/shard_map/inverse/pallas_call | solution.py:259
  56.3 1.7 %collective-permute-done.1.refs_2_ = f32[64,128]{1,0:T(8,128)S(1)} collective-permute-done((f32[64,128]{1,0:T(8,128)S(1)}, f32[64,128]{1,0:T(8,128)S(1)}, u32[]{:S(2)}, u32[]{:S(2)}) %collective-permute-start.1) | collective-permute-done | bytes 32800 | tf_op jit(solution)/shard_map/ppermute | solution.py:314
  58.0 0.2 fill.1
  58.2 0.0 copy-start
  58.2 0.0 copy-start.1
  58.2 0.0 copy-start.2
  58.2 0.0 copy-start.3
  58.3 31.1 %all_to_all.11 = f32[128,1,1536]{2,1,0:T(1,128)S(1)} all-to-all(f32[128,1,1536]{2,1,0:T(1,128)S(1)} %bitcast.6), channel_id=1, replica_groups=mesh['ctx'=16,'y'=4,'zh'=4,'core'=2] {'ctx','y','core'}, dimensions={0} | all-to-all | bytes 1572864 | tf_op jit(solution)/shard_map/all_to_all | solution.py:299
  89.3 0.0 copy-done
  89.3 0.0 copy-done.1
  89.3 0.0 copy-done.2
  89.3 0.0 copy-done.3
  89.4 1.1 %outputs.1 = (bf16[512,128]{1,0:T(8,128)(2,1)}, bf16[512,128]{1,0:T(8,128)(2,1)}, bf16[512,128]{1,0:T(8,128)(2,1)}, bf16[512,128]{1,0:T(8,128)(2,1)}, f32[512,128]{1,0:T(8,128)}) custom-call(f32[1536,128]{1,0:T(8,128)S(1)} %bitcast.5, bf16[512,128]{1,0:T(8,128)(2,1)S(1)} %copy-done, bf16[512,128]{1,0:T(8,128)(2,1)S(1)} %copy-done.1, ...), custom_call_target="tpu_custom_call" | custom-call | tf_op jit(solution)/shard_map/outputs/pallas_call | solution.py:286
  (1 shorter events, 0.0 us)
Async XLA Ops:
  0.6 34.9 %copy-start.4 = (bf16[512,256]{1,0:T(8,128)(2,1)S(1)}, bf16[512,256]{1,0:T(8,128)(2,1)}, u32[]{:S(2)}) copy-start(bf16[512,256]{1,0:T(8,128)(2,1)} %constant.24.clone.refs_4_.refs_2_) | copy-start | bytes 786436
  0.6 34.9 %copy-start.5 = (bf16[512,256]{1,0:T(8,128)(2,1)S(1)}, bf16[512,256]{1,0:T(8,128)(2,1)}, u32[]{:S(2)}) copy-start(bf16[512,256]{1,0:T(8,128)(2,1)} %constant.23.clone.refs_3_) | copy-start | bytes 786436
  0.7 34.9 %copy-start.6 = (f32[64,256]{1,0:T(8,128)S(1)}, f32[64,256]{1,0:T(8,128)}, u32[]{:S(2)}) copy-start(f32[64,256]{1,0:T(8,128)} %constant.22.clone.refs_2_.refs_1_) | copy-start | bytes 196612
  0.7 34.9 %copy-start.7 = (bf16[128,192]{1,0:T(8,128)(2,1)S(1)}, bf16[128,192]{1,0:T(8,128)(2,1)}, u32[]{:S(2)}) copy-start(bf16[128,192]{1,0:T(8,128)(2,1)} %constant.21.clone.refs_1_) | copy-start | bytes 147460
  0.7 34.9 %copy-start.8 = (bf16[64,384]{1,0:T(8,128)(2,1)S(1)}, bf16[64,384]{1,0:T(8,128)(2,1)}, u32[]{:S(2)}) copy-start(bf16[64,384]{1,0:T(8,128)(2,1)} %constant.25.clone.refs_5_.refs_3_) | copy-start | bytes 147460
  36.8 12.7 %collective-permute-start = (f32[64,128]{1,0:T(8,128)S(1)}, f32[64,128]{1,0:T(8,128)S(1)}, u32[]{:S(2)}, u32[]{:S(2)}) collective-permute-start(f32[64,128]{1,0:T(8,128)S(1)} %get-tuple-element.8), channel_id=1, source_target_pairs={{0,2},{2,0},{4,6},{6,4},{1,3},{3,1},{5,7},{7,5},{8,10},{10,8},{12,... | collective-permute-start | bytes 98312 | tf_op jit(solution)/shard_map/ppermute | solution.py:313
  49.4 8.6 %collective-permute-start.1 = (f32[64,128]{1,0:T(8,128)S(1)}, f32[64,128]{1,0:T(8,128)S(1)}, u32[]{:S(2)}, u32[]{:S(2)}) collective-permute-start(f32[64,128]{1,0:T(8,128)S(1)} %add.7.refs_1_), channel_id=1, source_target_pairs={{0,6},{6,0},{2,4},{4,2},{1,7},{7,1},{3,5},{5,3},{8,14},{14,8},{10,... | collective-permute-start | bytes 98312 | tf_op jit(solution)/shard_map/ppermute | solution.py:314
  58.2 31.1 %copy-start = (bf16[512,128]{1,0:T(8,128)(2,1)S(1)}, bf16[512,128]{1,0:T(8,128)(2,1)}, u32[]{:S(2)}) copy-start(bf16[512,128]{1,0:T(8,128)(2,1)} %refs_1_.5) | copy-start | bytes 393220
  58.2 31.1 %copy-start.1 = (bf16[512,128]{1,0:T(8,128)(2,1)S(1)}, bf16[512,128]{1,0:T(8,128)(2,1)}, u32[]{:S(2)}) copy-start(bf16[512,128]{1,0:T(8,128)(2,1)} %refs_2_.5) | copy-start | bytes 393220
  58.2 31.1 %copy-start.2 = (bf16[512,128]{1,0:T(8,128)(2,1)S(1)}, bf16[512,128]{1,0:T(8,128)(2,1)}, u32[]{:S(2)}) copy-start(bf16[512,128]{1,0:T(8,128)(2,1)} %refs_3_.5) | copy-start | bytes 393220
  58.2 31.1 %copy-start.3 = (bf16[512,128]{1,0:T(8,128)(2,1)S(1)}, bf16[512,128]{1,0:T(8,128)(2,1)}, u32[]{:S(2)}) copy-start(bf16[512,128]{1,0:T(8,128)(2,1)} %refs_4_.4) | copy-start | bytes 393220

commit v4 on v3

--- a/solution.py
+++ b/solution.py
@@ -293,6 +293,10 @@
     )(recv, query, key, value, cotangent)
 
 
+def by_core(*pairs):
+    return [(2 * a + core, 2 * b + core) for core in range(2) for a, b in pairs[core]]
+
+
 def exchange(rows):
     shape = rows.shape
     flat = rows.reshape(LANES, 1, -1)
@@ -310,8 +314,8 @@
     recv = exchange(pack(place, query, key, value, taps, cotangent))
     spec, terms = forward(blocks, chunks, recv, first_fwd, twist, second_fwd, second_inv, first_inv)
     send = inverse(blocks, chunks, spec, twist, second_inv, first_inv)
-    terms = terms + lax.ppermute(terms, "zh", PAIRS_NEAR)
-    send = fill(blocks, chunks, send, terms, lax.ppermute(terms, "zh", PAIRS_ROUND))
+    terms = terms + lax.ppermute(terms, ("zh", "core"), by_core(PAIRS_NEAR, PAIRS_ROUND))
+    send = fill(blocks, chunks, send, terms, lax.ppermute(terms, ("zh", "core"), by_core(PAIRS_ROUND, PAIRS_NEAR)))
     back = exchange(send)
     scale = 1.0 / math.sqrt(float(blocks * length * lax.axis_size(("y", "zh", "core"))))
     return outputs(scale, back, query, key, value, cotangent)

time: 90.7 us -> 90.3 us (level)
  waiting for transfers between devices: 5.49 us -> 2.05 us
  starting transfers between devices: 14.5 us -> 17.1 us
    ppermute x2, waiting for transfers between devices: 5.49 us -> 2.05 us  [the longest x1 1.29 us: on_device(): lax.ppermute(terms, ('zh', 'core'), by_core(PAIRS_NEAR, PAIRS_ROUND))]
    ppermute x2, starting transfers between devices: 14.5 us -> 17.1 us  [the longest x1 9.76 us: on_device(): lax.ppermute(terms, ('zh', 'core'), by_core(PAIRS_NEAR, PAIRS_ROUND))]
where the time goes in v4:
time: 90.3 us; the launch traced here: 90.1 us
  blocking collectives  64.9 us (72%)
  starting transfers between devices  17.1 us (19%)
  Pallas kernels  5.19 us (6%)
  waiting for transfers between devices  2.05 us (2%)
    all_to_all x2, blocking collectives, exchange(): return lax.all_to_all(flat, GROUP, 0, 0, tiled=True).reshape(shape)  64.9 us
    ppermute x1, starting transfers between devices, on_device(): lax.ppermute(terms, ('zh', 'core'), by_core(PAIRS_NEAR, PAIRS_ROUND))  9.76 us
    ppermute x1, starting transfers between devices, on_device(): lax.ppermute(terms, ('zh', 'core'), by_core(PAIRS_ROUND, PAIRS_NEAR))  7.3 us
  transfers between devices with their start and end apart: 2, of which 2 were waited for; matrix products, arithmetic and copies ran while one was open for 0% of the time, Pallas kernels for 1%

profile of v4, /device:TPU:1, one launch (start us, length us, event | category | flops | bytes accessed | tf_op | source)
XLA Modules:
  0.0 90.1 jit_solution(16446933538676082146)
XLA Ops:
  0.6 0.0 copy-start.4
  0.6 0.0 copy-start.5
  0.7 0.0 copy-start.6
  0.7 0.0 copy-start.7
  0.7 0.0 copy-start.8
  0.7 1.4 %pack.1 = f32[1152,128]{1,0:T(8,128)S(1)} custom-call(s32[1]{0:T(128)} %bitcast.refs_0_, bf16[512,128]{1,0:T(8,128)(2,1)} %refs_1_.5, bf16[512,128]{1,0:T(8,128)(2,1)} %refs_2_.5, bf16[512,128]{1,0:T(8,128)(2,1)} %refs_3_.5, f32[512,128]{1,0:T(8,128)} %refs_4_.3, bf16[512,128]{1,0:T(8,128)(2,1)} %refs_4_.4), custom_call_target="tpu_custom_call" | custom-call | tf_op jit(solution)/shard_map/pack/pallas_call | solution.py:229
  2.2 33.4 %all_to_all.10 = f32[128,1,1152]{2,1,0:T(1,128)S(1)} all-to-all(f32[128,1,1152]{2,1,0:T(1,128)S(1)} %bitcast.7), channel_id=1, replica_groups=mesh['ctx'=16,'y'=4,'zh'=4,'core'=2] {'ctx','y','core'}, dimensions={0} | all-to-all | bytes 1179648 | tf_op jit(solution)/shard_map/all_to_all | solution.py:303
  35.5 0.0 copy-done.4
  35.5 0.0 copy-done.5
  35.5 0.0 copy-done.6
  35.5 0.0 copy-done.7
  35.5 0.0 copy-done.8
  35.6 1.2 %forward.1 = (f32[1088,256]{1,0:T(8,128)S(1)}, f32[64,128]{1,0:T(8,128)S(1)}) custom-call(f32[1152,128]{1,0:T(8,128)S(1)} %bitcast.8, bf16[128,192]{1,0:T(8,128)(2,1)S(1)} %copy-done.7, f32[64,256]{1,0:T(8,128)S(1)} %copy-done.6, bf16[512,256]{1,0:T(8,128)(2,1)S(1)} %copy-done.5, bf16[512,256]{1,0:T(8,128)(2,1)S(1)} %copy-done.4, bf16[64,384]{1,0:T(8,128)(2,1)S(1)} %copy-done.8), custom_call_target="tpu_custom_call" | custom-call | tf_op jit(solution)/shard_map/forward/pallas_call | solution.py:243
  36.8 9.8 %collective-permute-start = (f32[64,128]{1,0:T(8,128)S(1)}, f32[64,128]{1,0:T(8,128)S(1)}, u32[]{:S(2)}, u32[]{:S(2)}) collective-permute-start(f32[64,128]{1,0:T(8,128)S(1)} %get-tuple-element.8), channel_id=1, source_target_pairs={{0,2},{2,0},{4,6},{6,4},{1,7},{7,1},{3,5},{5,3},{8,10},{10,8},{12,... | collective-permute-start | bytes 98312 | tf_op jit(solution)/shard_map/ppermute | solution.py:317
  46.5 1.3 %collective-permute-done = f32[64,128]{1,0:T(8,128)S(1)} collective-permute-done((f32[64,128]{1,0:T(8,128)S(1)}, f32[64,128]{1,0:T(8,128)S(1)}, u32[]{:S(2)}, u32[]{:S(2)}) %collective-permute-start) | collective-permute-done | bytes 32800 | tf_op jit(solution)/shard_map/ppermute | solution.py:317
  47.8 7.3 %collective-permute-start.1 = (f32[64,128]{1,0:T(8,128)S(1)}, f32[64,128]{1,0:T(8,128)S(1)}, u32[]{:S(2)}, u32[]{:S(2)}) collective-permute-start(f32[64,128]{1,0:T(8,128)S(1)} %add.7.refs_1_), channel_id=1, source_target_pairs={{0,6},{6,0},{2,4},{4,2},{1,3},{3,1},{5,7},{7,5},{8,14},{14,8},{10,... | collective-permute-start | bytes 98312 | tf_op jit(solution)/shard_map/ppermute | solution.py:318
  55.2 1.2 %inverse.1.refs_0_ = f32[1024,128]{1,0:T(8,128)S(1)} custom-call(f32[1088,256]{1,0:T(8,128)S(1)} %get-tuple-element.7.refs_0_, f32[64,256]{1,0:T(8,128)S(1)} %copy-done.6, bf16[512,256]{1,0:T(8,128)(2,1)S(1)} %copy-done.4, bf16[64,384]{1,0:T(8,128)(2,1)S(1)} %copy-done.8), custom_call_target="tpu_custom_call" | custom-call | flops 1000000000 | bytes 4000000 | tf_op jit(solution)/shard_map/inverse/pallas_call | solution.py:259
  56.4 0.8 collective-permute-done.1.refs_2_
  57.1 0.2 fill.1
  57.3 0.0 copy-start
  57.4 0.0 copy-start.1
  57.4 0.0 copy-start.2
  57.4 0.0 copy-start.3
  57.4 31.5 %all_to_all.11 = f32[128,1,1536]{2,1,0:T(1,128)S(1)} all-to-all(f32[128,1,1536]{2,1,0:T(1,128)S(1)} %bitcast.6), channel_id=1, replica_groups=mesh['ctx'=16,'y'=4,'zh'=4,'core'=2] {'ctx','y','core'}, dimensions={0} | all-to-all | bytes 1572864 | tf_op jit(solution)/shard_map/all_to_all | solution.py:303
  88.9 0.0 copy-done
  88.9 0.0 copy-done.1
  88.9 0.0 copy-done.2
  88.9 0.0 copy-done.3
  88.9 1.1 %outputs.1 = (bf16[512,128]{1,0:T(8,128)(2,1)}, bf16[512,128]{1,0:T(8,128)(2,1)}, bf16[512,128]{1,0:T(8,128)(2,1)}, bf16[512,128]{1,0:T(8,128)(2,1)}, f32[512,128]{1,0:T(8,128)}) custom-call(f32[1536,128]{1,0:T(8,128)S(1)} %bitcast.5, bf16[512,128]{1,0:T(8,128)(2,1)S(1)} %copy-done, bf16[512,128]{1,0:T(8,128)(2,1)S(1)} %copy-done.1, ...), custom_call_target="tpu_custom_call" | custom-call | tf_op jit(solution)/shard_map/outputs/pallas_call | solution.py:286
  (1 shorter events, 0.0 us)
Async XLA Ops:
  0.6 34.9 %copy-start.4 = (bf16[512,256]{1,0:T(8,128)(2,1)S(1)}, bf16[512,256]{1,0:T(8,128)(2,1)}, u32[]{:S(2)}) copy-start(bf16[512,256]{1,0:T(8,128)(2,1)} %constant.24.clone.refs_4_.refs_2_) | copy-start | bytes 786436
  0.6 34.9 %copy-start.5 = (bf16[512,256]{1,0:T(8,128)(2,1)S(1)}, bf16[512,256]{1,0:T(8,128)(2,1)}, u32[]{:S(2)}) copy-start(bf16[512,256]{1,0:T(8,128)(2,1)} %constant.23.clone.refs_3_) | copy-start | bytes 786436
  0.7 34.9 %copy-start.6 = (f32[64,256]{1,0:T(8,128)S(1)}, f32[64,256]{1,0:T(8,128)}, u32[]{:S(2)}) copy-start(f32[64,256]{1,0:T(8,128)} %constant.22.clone.refs_2_.refs_1_) | copy-start | bytes 196612
  0.7 34.9 %copy-start.7 = (bf16[128,192]{1,0:T(8,128)(2,1)S(1)}, bf16[128,192]{1,0:T(8,128)(2,1)}, u32[]{:S(2)}) copy-start(bf16[128,192]{1,0:T(8,128)(2,1)} %constant.21.clone.refs_1_) | copy-start | bytes 147460
  0.7 34.9 %copy-start.8 = (bf16[64,384]{1,0:T(8,128)(2,1)S(1)}, bf16[64,384]{1,0:T(8,128)(2,1)}, u32[]{:S(2)}) copy-start(bf16[64,384]{1,0:T(8,128)(2,1)} %constant.25.clone.refs_5_.refs_3_) | copy-start | bytes 147460
  36.8 11.1 %collective-permute-start = (f32[64,128]{1,0:T(8,128)S(1)}, f32[64,128]{1,0:T(8,128)S(1)}, u32[]{:S(2)}, u32[]{:S(2)}) collective-permute-start(f32[64,128]{1,0:T(8,128)S(1)} %get-tuple-element.8), channel_id=1, source_target_pairs={{0,2},{2,0},{4,6},{6,4},{1,7},{7,1},{3,5},{5,3},{8,10},{10,8},{12,... | collective-permute-start | bytes 98312 | tf_op jit(solution)/shard_map/ppermute | solution.py:317
  47.8 9.3 %collective-permute-start.1 = (f32[64,128]{1,0:T(8,128)S(1)}, f32[64,128]{1,0:T(8,128)S(1)}, u32[]{:S(2)}, u32[]{:S(2)}) collective-permute-start(f32[64,128]{1,0:T(8,128)S(1)} %add.7.refs_1_), channel_id=1, source_target_pairs={{0,6},{6,0},{2,4},{4,2},{1,3},{3,1},{5,7},{7,5},{8,14},{14,8},{10,... | collective-permute-start | bytes 98312 | tf_op jit(solution)/shard_map/ppermute | solution.py:318
  57.3 31.6 %copy-start = (bf16[512,128]{1,0:T(8,128)(2,1)S(1)}, bf16[512,128]{1,0:T(8,128)(2,1)}, u32[]{:S(2)}) copy-start(bf16[512,128]{1,0:T(8,128)(2,1)} %refs_1_.5) | copy-start | bytes 393220
  57.4 31.6 %copy-start.1 = (bf16[512,128]{1,0:T(8,128)(2,1)S(1)}, bf16[512,128]{1,0:T(8,128)(2,1)}, u32[]{:S(2)}) copy-start(bf16[512,128]{1,0:T(8,128)(2,1)} %refs_2_.5) | copy-start | bytes 393220
  57.4 31.6 %copy-start.2 = (bf16[512,128]{1,0:T(8,128)(2,1)S(1)}, bf16[512,128]{1,0:T(8,128)(2,1)}, u32[]{:S(2)}) copy-start(bf16[512,128]{1,0:T(8,128)(2,1)} %refs_3_.5) | copy-start | bytes 393220
  57.4 31.6 %copy-start.3 = (bf16[512,128]{1,0:T(8,128)(2,1)S(1)}, bf16[512,128]{1,0:T(8,128)(2,1)}, u32[]{:S(2)}) copy-start(bf16[512,128]{1,0:T(8,128)(2,1)} %refs_4_.4) | copy-start | bytes 393220

commit v5 on v4

--- a/solution.py
+++ b/solution.py
@@ -129,7 +129,10 @@
             place = pl.ds((start + offset) * first, first)
             high_ref[place, :] = high
             low_ref[place, :] = low
-    spec_ref[...] = second_stage(high_ref[...], low_ref[...], second_ref)
+        if (start + len(group)) % columns == 0 or len(group) == 1:
+            begin = start + len(group) - (columns if len(group) > 1 else 1)
+            done = pl.ds(begin * first, (start + len(group) - begin) * first)
+            spec_ref[done, :] = second_stage(high_ref[done, :], low_ref[done, :], second_ref)
     real = jnp.zeros((first, LANES), jnp.float32)
     imag = jnp.zeros((first, LANES), jnp.float32)
     for column in range(columns):

time: 90.3 us -> 90.3 us (level)
  no operation moved by 1% of the time
where the time goes in v5:
time: 90.3 us; the launch traced here: 90.1 us
  blocking collectives  64.9 us (72%)
  starting transfers between devices  17.1 us (19%)
  Pallas kernels  5.2 us (6%)
  waiting for transfers between devices  2.05 us (2%)
    all_to_all x2, blocking collectives, exchange(): return lax.all_to_all(flat, GROUP, 0, 0, tiled=True).reshape(shape)  64.9 us
    ppermute x1, starting transfers between devices, on_device(): lax.ppermute(terms, ('zh', 'core'), by_core(PAIRS_NEAR, PAIRS_ROUND))  9.76 us
    ppermute x1, starting transfers between devices, on_device(): lax.ppermute(terms, ('zh', 'core'), by_core(PAIRS_ROUND, PAIRS_NEAR))  7.3 us
  transfers between devices with their start and end apart: 2, of which 2 were waited for; matrix products, arithmetic and copies ran while one was open for 0% of the time, Pallas kernels for 1%

profile of v5, /device:TPU:1, one launch (start us, length us, event | category | flops | bytes accessed | tf_op | source)
XLA Modules:
  0.0 90.1 jit_solution(16595617690859887688)
XLA Ops:
  0.6 0.0 copy-start.4
  0.6 0.0 copy-start.5
  0.7 0.0 copy-start.6
  0.7 0.0 copy-start.7
  0.7 0.0 copy-start.8
  0.7 1.4 %pack.1 = f32[1152,128]{1,0:T(8,128)S(1)} custom-call(s32[1]{0:T(128)} %bitcast.refs_0_, bf16[512,128]{1,0:T(8,128)(2,1)} %refs_1_.5, bf16[512,128]{1,0:T(8,128)(2,1)} %refs_2_.5, bf16[512,128]{1,0:T(8,128)(2,1)} %refs_3_.5, f32[512,128]{1,0:T(8,128)} %refs_4_.3, bf16[512,128]{1,0:T(8,128)(2,1)} %refs_4_.4), custom_call_target="tpu_custom_call" | custom-call | tf_op jit(solution)/shard_map/pack/pallas_call | solution.py:232
  2.2 33.4 %all_to_all.10 = f32[128,1,1152]{2,1,0:T(1,128)S(1)} all-to-all(f32[128,1,1152]{2,1,0:T(1,128)S(1)} %bitcast.7), channel_id=1, replica_groups=mesh['ctx'=16,'y'=4,'zh'=4,'core'=2] {'ctx','y','core'}, dimensions={0} | all-to-all | bytes 1179648 | tf_op jit(solution)/shard_map/all_to_all | solution.py:306
  35.5 0.0 copy-done.4
  35.5 0.0 copy-done.5
  35.5 0.0 copy-done.6
  35.5 0.0 copy-done.7
  35.5 0.0 copy-done.8
  35.6 1.2 %forward.1 = (f32[1088,256]{1,0:T(8,128)S(1)}, f32[64,128]{1,0:T(8,128)S(1)}) custom-call(f32[1152,128]{1,0:T(8,128)S(1)} %bitcast.8, bf16[128,192]{1,0:T(8,128)(2,1)S(1)} %copy-done.7, f32[64,256]{1,0:T(8,128)S(1)} %copy-done.6, bf16[512,256]{1,0:T(8,128)(2,1)S(1)} %copy-done.5, bf16[512,256]{1,0:T(8,128)(2,1)S(1)} %copy-done.4, bf16[64,384]{1,0:T(8,128)(2,1)S(1)} %copy-done.8), custom_call_target="tpu_custom_call" | custom-call | tf_op jit(solution)/shard_map/forward/pallas_call | solution.py:246
  36.8 9.8 %collective-permute-start = (f32[64,128]{1,0:T(8,128)S(1)}, f32[64,128]{1,0:T(8,128)S(1)}, u32[]{:S(2)}, u32[]{:S(2)}) collective-permute-start(f32[64,128]{1,0:T(8,128)S(1)} %get-tuple-element.8), channel_id=1, source_target_pairs={{0,2},{2,0},{4,6},{6,4},{1,7},{7,1},{3,5},{5,3},{8,10},{10,8},{12,... | collective-permute-start | bytes 98312 | tf_op jit(solution)/shard_map/ppermute | solution.py:320
  46.6 1.3 %collective-permute-done = f32[64,128]{1,0:T(8,128)S(1)} collective-permute-done((f32[64,128]{1,0:T(8,128)S(1)}, f32[64,128]{1,0:T(8,128)S(1)}, u32[]{:S(2)}, u32[]{:S(2)}) %collective-permute-start) | collective-permute-done | bytes 32800 | tf_op jit(solution)/shard_map/ppermute | solution.py:320
  47.8 7.3 %collective-permute-start.1 = (f32[64,128]{1,0:T(8,128)S(1)}, f32[64,128]{1,0:T(8,128)S(1)}, u32[]{:S(2)}, u32[]{:S(2)}) collective-permute-start(f32[64,128]{1,0:T(8,128)S(1)} %add.7.refs_1_), channel_id=1, source_target_pairs={{0,6},{6,0},{2,4},{4,2},{1,3},{3,1},{5,7},{7,5},{8,14},{14,8},{10,... | collective-permute-start | bytes 98312 | tf_op jit(solution)/shard_map/ppermute | solution.py:321
  55.2 1.2 %inverse.1.refs_0_ = f32[1024,128]{1,0:T(8,128)S(1)} custom-call(f32[1088,256]{1,0:T(8,128)S(1)} %get-tuple-element.7.refs_0_, f32[64,256]{1,0:T(8,128)S(1)} %copy-done.6, bf16[512,256]{1,0:T(8,128)(2,1)S(1)} %copy-done.4, bf16[64,384]{1,0:T(8,128)(2,1)S(1)} %copy-done.8), custom_call_target="tpu_custom_call" | custom-call | flops 1000000000 | bytes 4000000 | tf_op jit(solution)/shard_map/inverse/pallas_call | solution.py:262
  56.4 0.8 collective-permute-done.1.refs_2_
  57.1 0.2 fill.1
  57.4 0.0 copy-start
  57.4 0.0 copy-start.1
  57.4 0.0 copy-start.2
  57.4 0.0 copy-start.3
  57.4 31.5 %all_to_all.11 = f32[128,1,1536]{2,1,0:T(1,128)S(1)} all-to-all(f32[128,1,1536]{2,1,0:T(1,128)S(1)} %bitcast.6), channel_id=1, replica_groups=mesh['ctx'=16,'y'=4,'zh'=4,'core'=2] {'ctx','y','core'}, dimensions={0} | all-to-all | bytes 1572864 | tf_op jit(solution)/shard_map/all_to_all | solution.py:306
  88.9 0.0 copy-done
  88.9 0.0 copy-done.1
  88.9 0.0 copy-done.2
  88.9 0.0 copy-done.3
  89.0 1.1 %outputs.1 = (bf16[512,128]{1,0:T(8,128)(2,1)}, bf16[512,128]{1,0:T(8,128)(2,1)}, bf16[512,128]{1,0:T(8,128)(2,1)}, bf16[512,128]{1,0:T(8,128)(2,1)}, f32[512,128]{1,0:T(8,128)}) custom-call(f32[1536,128]{1,0:T(8,128)S(1)} %bitcast.5, bf16[512,128]{1,0:T(8,128)(2,1)S(1)} %copy-done, bf16[512,128]{1,0:T(8,128)(2,1)S(1)} %copy-done.1, ...), custom_call_target="tpu_custom_call" | custom-call | tf_op jit(solution)/shard_map/outputs/pallas_call | solution.py:289
  (1 shorter events, 0.0 us)
Async XLA Ops:
  0.6 34.9 %copy-start.4 = (bf16[512,256]{1,0:T(8,128)(2,1)S(1)}, bf16[512,256]{1,0:T(8,128)(2,1)}, u32[]{:S(2)}) copy-start(bf16[512,256]{1,0:T(8,128)(2,1)} %constant.24.clone.refs_4_.refs_2_) | copy-start | bytes 786436
  0.6 34.9 %copy-start.5 = (bf16[512,256]{1,0:T(8,128)(2,1)S(1)}, bf16[512,256]{1,0:T(8,128)(2,1)}, u32[]{:S(2)}) copy-start(bf16[512,256]{1,0:T(8,128)(2,1)} %constant.23.clone.refs_3_) | copy-start | bytes 786436
  0.7 34.9 %copy-start.6 = (f32[64,256]{1,0:T(8,128)S(1)}, f32[64,256]{1,0:T(8,128)}, u32[]{:S(2)}) copy-start(f32[64,256]{1,0:T(8,128)} %constant.22.clone.refs_2_.refs_1_) | copy-start | bytes 196612
  0.7 34.9 %copy-start.7 = (bf16[128,192]{1,0:T(8,128)(2,1)S(1)}, bf16[128,192]{1,0:T(8,128)(2,1)}, u32[]{:S(2)}) copy-start(bf16[128,192]{1,0:T(8,128)(2,1)} %constant.21.clone.refs_1_) | copy-start | bytes 147460
  0.7 34.9 %copy-start.8 = (bf16[64,384]{1,0:T(8,128)(2,1)S(1)}, bf16[64,384]{1,0:T(8,128)(2,1)}, u32[]{:S(2)}) copy-start(bf16[64,384]{1,0:T(8,128)(2,1)} %constant.25.clone.refs_5_.refs_3_) | copy-start | bytes 147460
  36.8 11.1 %collective-permute-start = (f32[64,128]{1,0:T(8,128)S(1)}, f32[64,128]{1,0:T(8,128)S(1)}, u32[]{:S(2)}, u32[]{:S(2)}) collective-permute-start(f32[64,128]{1,0:T(8,128)S(1)} %get-tuple-element.8), channel_id=1, source_target_pairs={{0,2},{2,0},{4,6},{6,4},{1,7},{7,1},{3,5},{5,3},{8,10},{10,8},{12,... | collective-permute-start | bytes 98312 | tf_op jit(solution)/shard_map/ppermute | solution.py:320
  47.8 9.3 %collective-permute-start.1 = (f32[64,128]{1,0:T(8,128)S(1)}, f32[64,128]{1,0:T(8,128)S(1)}, u32[]{:S(2)}, u32[]{:S(2)}) collective-permute-start(f32[64,128]{1,0:T(8,128)S(1)} %add.7.refs_1_), channel_id=1, source_target_pairs={{0,6},{6,0},{2,4},{4,2},{1,3},{3,1},{5,7},{7,5},{8,14},{14,8},{10,... | collective-permute-start | bytes 98312 | tf_op jit(solution)/shard_map/ppermute | solution.py:321
  57.4 31.6 %copy-start = (bf16[512,128]{1,0:T(8,128)(2,1)S(1)}, bf16[512,128]{1,0:T(8,128)(2,1)}, u32[]{:S(2)}) copy-start(bf16[512,128]{1,0:T(8,128)(2,1)} %refs_1_.5) | copy-start | bytes 393220
  57.4 31.6 %copy-start.1 = (bf16[512,128]{1,0:T(8,128)(2,1)S(1)}, bf16[512,128]{1,0:T(8,128)(2,1)}, u32[]{:S(2)}) copy-start(bf16[512,128]{1,0:T(8,128)(2,1)} %refs_2_.5) | copy-start | bytes 393220
  57.4 31.6 %copy-start.2 = (bf16[512,128]{1,0:T(8,128)(2,1)S(1)}, bf16[512,128]{1,0:T(8,128)(2,1)}, u32[]{:S(2)}) copy-start(bf16[512,128]{1,0:T(8,128)(2,1)} %refs_3_.5) | copy-start | bytes 393220
  57.4 31.6 %copy-start.3 = (bf16[512,128]{1,0:T(8,128)(2,1)S(1)}, bf16[512,128]{1,0:T(8,128)(2,1)}, u32[]{:S(2)}) copy-start(bf16[512,128]{1,0:T(8,128)(2,1)} %refs_4_.4) | copy-start | bytes 393220

commit v6 on v4

--- a/solution.py
+++ b/solution.py
@@ -108,19 +108,10 @@
             [recv_ref[pl.ds(column * rows + signal * chunks + chunk, blocks, stride=stride), :] for chunk in range(chunks)], 0
         )
 
-    taps = jnp.concatenate(
-        [
-            recv_ref[pl.ds(2 * chunk * rows + rows - 1, blocks, stride=stride), :]
-            + recv_ref[pl.ds((2 * chunk + 1) * rows + rows - 1, blocks, stride=stride), :]
-            for chunk in range(chunks)
-        ],
-        0,
-    )
-    signals = [read(column, signal) for signal in range(2) for column in range(columns)] + [taps]
+    signals = [read(column, signal) for signal in range(2) for column in range(columns)]
     for start in range(0, len(signals), 2):
         group = signals[start : start + 2]
-        wide = jnp.concatenate(group, 1) if len(group) > 1 else group[0]
-        high, low = split(wide)
+        high, low = split(jnp.concatenate(group, 1))
         mixed = dot(first_ref[...], jnp.concatenate([high, low, high], 0))
         for offset in range(len(group)):
             lanes = slice(offset * LANES, (offset + 1) * LANES)
@@ -129,7 +120,9 @@
             place = pl.ds((start + offset) * first, first)
             high_ref[place, :] = high
             low_ref[place, :] = low
-    spec_ref[...] = second_stage(high_ref[...], low_ref[...], second_ref)
+        if (start + len(group)) % columns == 0:
+            done = pl.ds((start + len(group) - columns) * first, columns * first)
+            spec_ref[done, :] = second_stage(high_ref[done, :], low_ref[done, :], second_ref)
     real = jnp.zeros((first, LANES), jnp.float32)
     imag = jnp.zeros((first, LANES), jnp.float32)
     for column in range(columns):
@@ -146,13 +139,29 @@
     terms_ref[...] = dot(first_inv_ref[...], jnp.concatenate([high, low, high], 0))
 
 
-def inverse_kernel(blocks, chunks, spec_ref, twist_ref, inverse_ref, first_inv_ref, send_ref, high_ref, low_ref):
+def inverse_kernel(
+    blocks, chunks, recv_ref, spec_ref, first_ref, twist_ref, second_ref, inverse_ref, first_inv_ref, send_ref, high_ref, low_ref
+):
     first = blocks * chunks
     columns = 2 * chunks
     cosine = twist_ref[:, :LANES]
     sine = twist_ref[:, LANES:]
-    taps = pl.ds(2 * columns * first, first)
-    taps_real, taps_imag = spec_ref[taps, :LANES], spec_ref[taps, LANES:]
+    rows = 2 * chunks + 1
+    stride = columns * rows
+    taps = jnp.concatenate(
+        [
+            recv_ref[pl.ds(2 * chunk * rows + rows - 1, blocks, stride=stride), :]
+            + recv_ref[pl.ds((2 * chunk + 1) * rows + rows - 1, blocks, stride=stride), :]
+            for chunk in range(chunks)
+        ],
+        0,
+    )
+    high, low = split(taps)
+    mixed = dot(first_ref[...], jnp.concatenate([high, low, high], 0))
+    real, imag = mixed[:first, :], mixed[first:, :]
+    high, low = split(jnp.concatenate([real * cosine - imag * sine, imag * cosine + real * sine], 1))
+    taps_spec = second_stage(high, low, second_ref)
+    taps_real, taps_imag = taps_spec[:, :LANES], taps_spec[:, LANES:]
     for column in range(columns):
         place = pl.ds(column * first, first)
         real, imag = spec_ref[place, :LANES], spec_ref[place, LANES:]
@@ -239,7 +248,7 @@
 
 def forward(blocks, chunks, recv, first_fwd, twist, second_fwd, second_inv, first_inv):
     first = blocks * chunks
-    count = (4 * chunks + 1) * first
+    count = 4 * chunks * first
     return pl.pallas_call(
         lambda *refs: forward_kernel(blocks, chunks, *refs),
         out_shape=(
@@ -254,18 +263,18 @@
     )(recv, first_fwd, twist, second_fwd, second_inv, first_inv)
 
 
-def inverse(blocks, chunks, spec, twist, second_inv, first_inv):
+def inverse(blocks, chunks, recv, spec, first_fwd, twist, second_fwd, second_inv, first_inv):
     count = 4 * chunks * blocks * chunks
     return pl.pallas_call(
         lambda *refs: inverse_kernel(blocks, chunks, *refs),
         out_shape=jax.ShapeDtypeStruct((LANES * 2 * chunks, LANES), jnp.float32),
-        in_specs=whole(4),
+        in_specs=whole(7),
         out_specs=whole(1)[0],
         scratch_shapes=[pltpu.VMEM((count, 2 * LANES), jnp.bfloat16)] * 2,
         compiler_params=params(),
         cost_estimate=pl.CostEstimate(flops=10**9, bytes_accessed=4 * 10**6, transcendentals=0),
         name="inverse",
-    )(spec, twist, second_inv, first_inv)
+    )(recv, spec, first_fwd, twist, second_fwd, second_inv, first_inv)
 
 
 def fill(blocks, chunks, send, *terms):
@@ -313,7 +322,7 @@
     place = lax.axis_index(("y", "core")).astype(jnp.int32).reshape(1)
     recv = exchange(pack(place, query, key, value, taps, cotangent))
     spec, terms = forward(blocks, chunks, recv, first_fwd, twist, second_fwd, second_inv, first_inv)
-    send = inverse(blocks, chunks, spec, twist, second_inv, first_inv)
+    send = inverse(blocks, chunks, recv, spec, first_fwd, twist, second_fwd, second_inv, first_inv)
     terms = terms + lax.ppermute(terms, ("zh", "core"), by_core(PAIRS_NEAR, PAIRS_ROUND))
     send = fill(blocks, chunks, send, terms, lax.ppermute(terms, ("zh", "core"), by_core(PAIRS_ROUND, PAIRS_NEAR)))
     back = exchange(send)

time: 90.3 us -> 90.4 us (level)
  transfers between devices with their start and end apart: 2 -> 2, of which waited for: 2 -> 2; matrix products, arithmetic and copies ran while one was open for 0% -> 0% of each run, Pallas kernels for 1% -> 2%
where the time goes in v6:
time: 90.4 us; the launch traced here: 90.1 us
  blocking collectives  65 us (72%)
  starting transfers between devices  17.1 us (19%)
  Pallas kernels  5.49 us (6%)
  waiting for transfers between devices  1.66 us (2%)
    all_to_all x2, blocking collectives, exchange(): return lax.all_to_all(flat, GROUP, 0, 0, tiled=True).reshape(shape)  65 us
    ppermute x1, starting transfers between devices, on_device(): lax.ppermute(terms, ('zh', 'core'), by_core(PAIRS_NEAR, PAIRS_ROUND))  9.76 us
    ppermute x1, starting transfers between devices, on_device(): lax.ppermute(terms, ('zh', 'core'), by_core(PAIRS_ROUND, PAIRS_NEAR))  7.3 us
  transfers between devices with their start and end apart: 2, of which 2 were waited for; matrix products, arithmetic and copies ran while one was open for 0% of the time, Pallas kernels for 2%

profile of v6, /device:TPU:1, one launch (start us, length us, event | category | flops | bytes accessed | tf_op | source)
XLA Modules:
  0.0 90.1 jit_solution(5239996115070879041)
XLA Ops:
  0.6 1.4 %pack.1 = f32[1152,128]{1,0:T(8,128)S(1)} custom-call(s32[1]{0:T(128)} %bitcast.refs_0_, bf16[512,128]{1,0:T(8,128)(2,1)} %refs_1_.4, bf16[512,128]{1,0:T(8,128)(2,1)} %refs_2_.5, bf16[512,128]{1,0:T(8,128)(2,1)} %refs_3_.5, f32[512,128]{1,0:T(8,128)} %refs_4_.4, bf16[512,128]{1,0:T(8,128)(2,1)} %refs_4_.5), custom_call_target="tpu_custom_call" | custom-call | tf_op jit(solution)/shard_map/pack/pallas_call | solution.py:238
  2.0 0.0 copy-start.4
  2.0 0.0 copy-start.5
  2.1 0.0 copy-start.6
  2.1 0.0 copy-start.7
  2.1 0.0 copy-start.8
  2.1 33.5 %all_to_all.10 = f32[128,1,1152]{2,1,0:T(1,128)S(1)} all-to-all(f32[128,1,1152]{2,1,0:T(1,128)S(1)} %bitcast.7), channel_id=1, replica_groups=mesh['ctx'=16,'y'=4,'zh'=4,'core'=2] {'ctx','y','core'}, dimensions={0} | all-to-all | bytes 1179648 | tf_op jit(solution)/shard_map/all_to_all | solution.py:312
  35.6 0.0 copy-done.4
  35.6 0.0 copy-done.5
  35.6 0.0 copy-done.6
  35.6 0.0 copy-done.7
  35.6 0.0 copy-done.8
  35.6 1.2 %forward.1 = (f32[1024,256]{1,0:T(8,128)S(1)}, f32[64,128]{1,0:T(8,128)S(1)}) custom-call(f32[1152,128]{1,0:T(8,128)S(1)} %bitcast.8, bf16[128,192]{1,0:T(8,128)(2,1)S(1)} %copy-done.7, f32[64,256]{1,0:T(8,128)S(1)} %copy-done.6, bf16[512,256]{1,0:T(8,128)(2,1)S(1)} %copy-done.5, bf16[512,256]{1,0:T(8,128)(2,1)S(1)} %copy-done.4, bf16[64,384]{1,0:T(8,128)(2,1)S(1)} %copy-done.8), custom_call_target="tpu_custom_call" | custom-call | tf_op jit(solution)/shard_map/forward/pallas_call | solution.py:252
  36.8 9.8 %collective-permute-start = (f32[64,128]{1,0:T(8,128)S(1)}, f32[64,128]{1,0:T(8,128)S(1)}, u32[]{:S(2)}, u32[]{:S(2)}) collective-permute-start(f32[64,128]{1,0:T(8,128)S(1)} %get-tuple-element.8), channel_id=1, source_target_pairs={{0,2},{2,0},{4,6},{6,4},{1,7},{7,1},{3,5},{5,3},{8,10},{10,8},{12,... | collective-permute-start | bytes 98312 | tf_op jit(solution)/shard_map/ppermute | solution.py:326
  46.6 1.3 %collective-permute-done = f32[64,128]{1,0:T(8,128)S(1)} collective-permute-done((f32[64,128]{1,0:T(8,128)S(1)}, f32[64,128]{1,0:T(8,128)S(1)}, u32[]{:S(2)}, u32[]{:S(2)}) %collective-permute-start) | collective-permute-done | bytes 32800 | tf_op jit(solution)/shard_map/ppermute | solution.py:326
  47.9 7.3 %collective-permute-start.1 = (f32[64,128]{1,0:T(8,128)S(1)}, f32[64,128]{1,0:T(8,128)S(1)}, u32[]{:S(2)}, u32[]{:S(2)}) collective-permute-start(f32[64,128]{1,0:T(8,128)S(1)} %add.7.refs_1_), channel_id=1, source_target_pairs={{0,6},{6,0},{2,4},{4,2},{1,3},{3,1},{5,7},{7,5},{8,14},{14,8},{10,... | collective-permute-start | bytes 98312 | tf_op jit(solution)/shard_map/ppermute | solution.py:327
  55.2 1.6 %inverse.1.refs_0_ = f32[1024,128]{1,0:T(8,128)S(1)} custom-call(f32[1152,128]{1,0:T(8,128)S(1)} %bitcast.9, f32[1024,256]{1,0:T(8,128)S(1)} %get-tuple-element.7.refs_1_, bf16[128,192]{1,0:T(8,128)(2,1)S(1)} %copy-done.7, f32[64,256]{1,0:T(8,128)S(1)} %copy-done.6, bf16[512,256]{1,0:T(8,128)(2,1)S(1)} %copy-done.5, bf16[512,256]{1,0:T(8,128)(2,1)S(1)} %copy-done.4, ...), custom_call_target="tpu_custom_call" | custom-call | flops 1000000000 | bytes 4000000 | tf_op jit(solution)/shard_map/inverse/pallas_call | solution.py:268
  56.8 0.4 collective-permute-done.1.refs_2_
  57.2 0.2 fill.1
  57.4 0.0 copy-start
  57.4 0.0 copy-start.1
  57.4 0.0 copy-start.2
  57.4 0.0 copy-start.3
  57.4 31.5 %all_to_all.11 = f32[128,1,1536]{2,1,0:T(1,128)S(1)} all-to-all(f32[128,1,1536]{2,1,0:T(1,128)S(1)} %bitcast.6), channel_id=1, replica_groups=mesh['ctx'=16,'y'=4,'zh'=4,'core'=2] {'ctx','y','core'}, dimensions={0} | all-to-all | bytes 1572864 | tf_op jit(solution)/shard_map/all_to_all | solution.py:312
  89.0 0.0 copy-done
  89.0 0.0 copy-done.1
  89.0 0.0 copy-done.2
  89.0 0.0 copy-done.3
  89.0 1.1 %outputs.1 = (bf16[512,128]{1,0:T(8,128)(2,1)}, bf16[512,128]{1,0:T(8,128)(2,1)}, bf16[512,128]{1,0:T(8,128)(2,1)}, bf16[512,128]{1,0:T(8,128)(2,1)}, f32[512,128]{1,0:T(8,128)}) custom-call(f32[1536,128]{1,0:T(8,128)S(1)} %bitcast.5, bf16[512,128]{1,0:T(8,128)(2,1)S(1)} %copy-done, bf16[512,128]{1,0:T(8,128)(2,1)S(1)} %copy-done.1, ...), custom_call_target="tpu_custom_call" | custom-call | tf_op jit(solution)/shard_map/outputs/pallas_call | solution.py:295
  (1 shorter events, 0.0 us)
Async XLA Ops:
  2.0 33.6 %copy-start.4 = (bf16[512,256]{1,0:T(8,128)(2,1)S(1)}, bf16[512,256]{1,0:T(8,128)(2,1)}, u32[]{:S(2)}) copy-start(bf16[512,256]{1,0:T(8,128)(2,1)} %constant.24.clone.refs_4_.refs_5_) | copy-start | bytes 786436
  2.0 33.6 %copy-start.5 = (bf16[512,256]{1,0:T(8,128)(2,1)S(1)}, bf16[512,256]{1,0:T(8,128)(2,1)}, u32[]{:S(2)}) copy-start(bf16[512,256]{1,0:T(8,128)(2,1)} %constant.23.clone.refs_3_.refs_4_) | copy-start | bytes 786436
  2.1 33.5 %copy-start.6 = (f32[64,256]{1,0:T(8,128)S(1)}, f32[64,256]{1,0:T(8,128)}, u32[]{:S(2)}) copy-start(f32[64,256]{1,0:T(8,128)} %constant.22.clone.refs_2_.refs_3_) | copy-start | bytes 196612
  2.1 33.5 %copy-start.7 = (bf16[128,192]{1,0:T(8,128)(2,1)S(1)}, bf16[128,192]{1,0:T(8,128)(2,1)}, u32[]{:S(2)}) copy-start(bf16[128,192]{1,0:T(8,128)(2,1)} %constant.21.clone.refs_1_.refs_2_) | copy-start | bytes 147460
  2.1 33.5 %copy-start.8 = (bf16[64,384]{1,0:T(8,128)(2,1)S(1)}, bf16[64,384]{1,0:T(8,128)(2,1)}, u32[]{:S(2)}) copy-start(bf16[64,384]{1,0:T(8,128)(2,1)} %constant.25.clone.refs_5_.refs_6_) | copy-start | bytes 147460
  36.8 11.1 %collective-permute-start = (f32[64,128]{1,0:T(8,128)S(1)}, f32[64,128]{1,0:T(8,128)S(1)}, u32[]{:S(2)}, u32[]{:S(2)}) collective-permute-start(f32[64,128]{1,0:T(8,128)S(1)} %get-tuple-element.8), channel_id=1, source_target_pairs={{0,2},{2,0},{4,6},{6,4},{1,7},{7,1},{3,5},{5,3},{8,10},{10,8},{12,... | collective-permute-start | bytes 98312 | tf_op jit(solution)/shard_map/ppermute | solution.py:326
  47.9 9.3 %collective-permute-start.1 = (f32[64,128]{1,0:T(8,128)S(1)}, f32[64,128]{1,0:T(8,128)S(1)}, u32[]{:S(2)}, u32[]{:S(2)}) collective-permute-start(f32[64,128]{1,0:T(8,128)S(1)} %add.7.refs_1_), channel_id=1, source_target_pairs={{0,6},{6,0},{2,4},{4,2},{1,3},{3,1},{5,7},{7,5},{8,14},{14,8},{10,... | collective-permute-start | bytes 98312 | tf_op jit(solution)/shard_map/ppermute | solution.py:327
  57.4 31.6 %copy-start = (bf16[512,128]{1,0:T(8,128)(2,1)S(1)}, bf16[512,128]{1,0:T(8,128)(2,1)}, u32[]{:S(2)}) copy-start(bf16[512,128]{1,0:T(8,128)(2,1)} %refs_1_.4) | copy-start | bytes 393220
  57.4 31.6 %copy-start.1 = (bf16[512,128]{1,0:T(8,128)(2,1)S(1)}, bf16[512,128]{1,0:T(8,128)(2,1)}, u32[]{:S(2)}) copy-start(bf16[512,128]{1,0:T(8,128)(2,1)} %refs_2_.5) | copy-start | bytes 393220
  57.4 31.6 %copy-start.2 = (bf16[512,128]{1,0:T(8,128)(2,1)S(1)}, bf16[512,128]{1,0:T(8,128)(2,1)}, u32[]{:S(2)}) copy-start(bf16[512,128]{1,0:T(8,128)(2,1)} %refs_3_.5) | copy-start | bytes 393220
  57.4 31.6 %copy-start.3 = (bf16[512,128]{1,0:T(8,128)(2,1)S(1)}, bf16[512,128]{1,0:T(8,128)(2,1)}, u32[]{:S(2)}) copy-start(bf16[512,128]{1,0:T(8,128)(2,1)} %refs_4_.5) | copy-start | bytes 393220

commit v7 on v6

--- a/solution.py
+++ b/solution.py
@@ -323,7 +323,9 @@
     recv = exchange(pack(place, query, key, value, taps, cotangent))
     spec, terms = forward(blocks, chunks, recv, first_fwd, twist, second_fwd, second_inv, first_inv)
     send = inverse(blocks, chunks, recv, spec, first_fwd, twist, second_fwd, second_inv, first_inv)
-    terms = terms + lax.ppermute(terms, ("zh", "core"), by_core(PAIRS_NEAR, PAIRS_ROUND))
+    near = lax.ppermute(terms, ("zh", "core"), by_core(PAIRS_NEAR, PAIRS_ROUND))
+    near, send = lax.optimization_barrier((near, send))
+    terms = terms + near
     send = fill(blocks, chunks, send, terms, lax.ppermute(terms, ("zh", "core"), by_core(PAIRS_ROUND, PAIRS_NEAR)))
     back = exchange(send)
     scale = 1.0 / math.sqrt(float(blocks * length * lax.axis_size(("y", "zh", "core"))))

time: 90.4 us -> 90.4 us (level)
  waiting for transfers between devices: 1.66 us -> 2.6 us
    ppermute x1, waiting for transfers between devices: 0.37 us -> 2.59 us  [on_device(): lax.ppermute(terms, ('zh', 'core'), by_core(PAIRS_ROUND, PAIRS_NEAR))]
    ppermute x1, waiting for transfers between devices: 1.29 us -> 0.01 us  [on_device(): near = lax.ppermute(terms, ('zh', 'core'), by_core(PAIRS_NEAR, PAIRS_ROUND))]
  transfers between devices with their start and end apart: 2 -> 2, of which waited for: 2 -> 1; matrix products, arithmetic and copies ran while one was open for 0% -> 0% of each run, Pallas kernels for 2% -> 2%
where the time goes in v7:
time: 90.4 us; the launch traced here: 90.1 us
  blocking collectives  64.4 us (71%)
  starting transfers between devices  16.7 us (18%)
  Pallas kernels  5.49 us (6%)
  waiting for transfers between devices  2.6 us (3%)
    all_to_all x2, blocking collectives, exchange(): return lax.all_to_all(flat, GROUP, 0, 0, tiled=True).reshape(shape)  64.4 us
    ppermute x1, starting transfers between devices, on_device(): near = lax.ppermute(terms, ('zh', 'core'), by_core(PAIRS_NEAR, PAIRS_ROUND))  9.76 us
    ppermute x1, starting transfers between devices, on_device(): lax.ppermute(terms, ('zh', 'core'), by_core(PAIRS_ROUND, PAIRS_NEAR))  6.95 us
    ppermute x1, waiting for transfers between devices, on_device(): lax.ppermute(terms, ('zh', 'core'), by_core(PAIRS_ROUND, PAIRS_NEAR))  2.59 us
  transfers between devices with their start and end apart: 2, of which 1 were waited for; matrix products, arithmetic and copies ran while one was open for 0% of the time, Pallas kernels for 2%

profile of v7, /device:TPU:1, one launch (start us, length us, event | category | flops | bytes accessed | tf_op | source)
XLA Modules:
  0.0 90.1 jit_solution(17834183721877557907)
XLA Ops:
  0.6 1.4 %pack.1 = f32[1152,128]{1,0:T(8,128)S(1)} custom-call(s32[1]{0:T(128)} %bitcast.refs_0_, bf16[512,128]{1,0:T(8,128)(2,1)} %refs_1_.4, bf16[512,128]{1,0:T(8,128)(2,1)} %refs_2_.5, bf16[512,128]{1,0:T(8,128)(2,1)} %refs_3_.5, f32[512,128]{1,0:T(8,128)} %refs_4_.4, bf16[512,128]{1,0:T(8,128)(2,1)} %refs_4_.5), custom_call_target="tpu_custom_call" | custom-call | tf_op jit(solution)/shard_map/pack/pallas_call | solution.py:238
  2.0 0.0 copy-start.4
  2.0 0.0 copy-start.5
  2.1 0.0 copy-start.6
  2.1 0.0 copy-start.7
  2.1 0.0 copy-start.8
  2.1 33.5 %all_to_all.10 = f32[128,1,1152]{2,1,0:T(1,128)S(1)} all-to-all(f32[128,1,1152]{2,1,0:T(1,128)S(1)} %bitcast.7), channel_id=1, replica_groups=mesh['ctx'=16,'y'=4,'zh'=4,'core'=2] {'ctx','y','core'}, dimensions={0} | all-to-all | bytes 1179648 | tf_op jit(solution)/shard_map/all_to_all | solution.py:312
  35.6 0.0 copy-done.4
  35.6 0.0 copy-done.5
  35.6 0.0 copy-done.6
  35.6 0.0 copy-done.7
  35.6 0.0 copy-done.8
  35.6 1.2 %forward.1 = (f32[1024,256]{1,0:T(8,128)S(1)}, f32[64,128]{1,0:T(8,128)S(1)}) custom-call(f32[1152,128]{1,0:T(8,128)S(1)} %bitcast.8, bf16[128,192]{1,0:T(8,128)(2,1)S(1)} %copy-done.7, f32[64,256]{1,0:T(8,128)S(1)} %copy-done.6, bf16[512,256]{1,0:T(8,128)(2,1)S(1)} %copy-done.5, bf16[512,256]{1,0:T(8,128)(2,1)S(1)} %copy-done.4, bf16[64,384]{1,0:T(8,128)(2,1)S(1)} %copy-done.8), custom_call_target="tpu_custom_call" | custom-call | tf_op jit(solution)/shard_map/forward/pallas_call | solution.py:252
  36.8 9.8 %collective-permute-start = (f32[64,128]{1,0:T(8,128)S(1)}, f32[64,128]{1,0:T(8,128)S(1)}, u32[]{:S(2)}, u32[]{:S(2)}) collective-permute-start(f32[64,128]{1,0:T(8,128)S(1)} %get-tuple-element.9), channel_id=1, source_target_pairs={{0,2},{2,0},{4,6},{6,4},{1,7},{7,1},{3,5},{5,3},{8,10},{10,8},{12,... | collective-permute-start | bytes 98312 | tf_op jit(solution)/shard_map/ppermute | solution.py:326
  46.6 1.6 %inverse.1.refs_0_ = f32[1024,128]{1,0:T(8,128)S(1)} custom-call(f32[1152,128]{1,0:T(8,128)S(1)} %bitcast.9, f32[1024,256]{1,0:T(8,128)S(1)} %get-tuple-element.10.refs_1_, bf16[128,192]{1,0:T(8,128)(2,1)S(1)} %copy-done.7, f32[64,256]{1,0:T(8,128)S(1)} %copy-done.6, bf16[512,256]{1,0:T(8,128)(2,1)S(1)} %copy-done.5, bf16[512,256]{1,0:T(8,128)(2,1)S(1)} %copy-done.4, ...), custom_call_target="tpu_custom_call" | custom-call | flops 1000000000 | bytes 4000000 | tf_op jit(solution)/shard_map/inverse/pallas_call | solution.py:268
  48.2 0.0 collective-permute-done
  48.2 6.9 %collective-permute-start.1 = (f32[64,128]{1,0:T(8,128)S(1)}, f32[64,128]{1,0:T(8,128)S(1)}, u32[]{:S(2)}, u32[]{:S(2)}) collective-permute-start(f32[64,128]{1,0:T(8,128)S(1)} %add.7.refs_1_), channel_id=1, source_target_pairs={{0,6},{6,0},{2,4},{4,2},{1,3},{3,1},{5,7},{7,5},{8,14},{14,8},{10,... | collective-permute-start | bytes 98312 | tf_op jit(solution)/shard_map/ppermute | solution.py:329
  55.2 2.6 %collective-permute-done.1.refs_2_ = f32[64,128]{1,0:T(8,128)S(1)} collective-permute-done((f32[64,128]{1,0:T(8,128)S(1)}, f32[64,128]{1,0:T(8,128)S(1)}, u32[]{:S(2)}, u32[]{:S(2)}) %collective-permute-start.1) | collective-permute-done | bytes 32800 | tf_op jit(solution)/shard_map/ppermute | solution.py:329
  57.8 0.2 fill.1
  58.0 0.0 copy-start
  58.0 0.0 copy-start.1
  58.0 0.0 copy-start.2
  58.0 0.0 copy-start.3
  58.0 30.9 %all_to_all.11 = f32[128,1,1536]{2,1,0:T(1,128)S(1)} all-to-all(f32[128,1,1536]{2,1,0:T(1,128)S(1)} %bitcast.6), channel_id=1, replica_groups=mesh['ctx'=16,'y'=4,'zh'=4,'core'=2] {'ctx','y','core'}, dimensions={0} | all-to-all | bytes 1572864 | tf_op jit(solution)/shard_map/all_to_all | solution.py:312
  89.0 0.0 copy-done
  89.0 0.0 copy-done.1
  89.0 0.0 copy-done.2
  89.0 0.0 copy-done.3
  89.0 1.1 %outputs.1 = (bf16[512,128]{1,0:T(8,128)(2,1)}, bf16[512,128]{1,0:T(8,128)(2,1)}, bf16[512,128]{1,0:T(8,128)(2,1)}, bf16[512,128]{1,0:T(8,128)(2,1)}, f32[512,128]{1,0:T(8,128)}) custom-call(f32[1536,128]{1,0:T(8,128)S(1)} %bitcast.5, bf16[512,128]{1,0:T(8,128)(2,1)S(1)} %copy-done, bf16[512,128]{1,0:T(8,128)(2,1)S(1)} %copy-done.1, ...), custom_call_target="tpu_custom_call" | custom-call | tf_op jit(solution)/shard_map/outputs/pallas_call | solution.py:295
  (1 shorter events, 0.0 us)
Async XLA Ops:
  2.0 33.6 %copy-start.4 = (bf16[512,256]{1,0:T(8,128)(2,1)S(1)}, bf16[512,256]{1,0:T(8,128)(2,1)}, u32[]{:S(2)}) copy-start(bf16[512,256]{1,0:T(8,128)(2,1)} %constant.24.clone.refs_4_.refs_5_) | copy-start | bytes 786436
  2.0 33.6 %copy-start.5 = (bf16[512,256]{1,0:T(8,128)(2,1)S(1)}, bf16[512,256]{1,0:T(8,128)(2,1)}, u32[]{:S(2)}) copy-start(bf16[512,256]{1,0:T(8,128)(2,1)} %constant.23.clone.refs_3_.refs_4_) | copy-start | bytes 786436
  2.1 33.5 %copy-start.6 = (f32[64,256]{1,0:T(8,128)S(1)}, f32[64,256]{1,0:T(8,128)}, u32[]{:S(2)}) copy-start(f32[64,256]{1,0:T(8,128)} %constant.22.clone.refs_2_.refs_3_) | copy-start | bytes 196612
  2.1 33.5 %copy-start.7 = (bf16[128,192]{1,0:T(8,128)(2,1)S(1)}, bf16[128,192]{1,0:T(8,128)(2,1)}, u32[]{:S(2)}) copy-start(bf16[128,192]{1,0:T(8,128)(2,1)} %constant.21.clone.refs_1_.refs_2_) | copy-start | bytes 147460
  2.1 33.5 %copy-start.8 = (bf16[64,384]{1,0:T(8,128)(2,1)S(1)}, bf16[64,384]{1,0:T(8,128)(2,1)}, u32[]{:S(2)}) copy-start(bf16[64,384]{1,0:T(8,128)(2,1)} %constant.25.clone.refs_5_.refs_6_) | copy-start | bytes 147460
  36.8 11.4 %collective-permute-start = (f32[64,128]{1,0:T(8,128)S(1)}, f32[64,128]{1,0:T(8,128)S(1)}, u32[]{:S(2)}, u32[]{:S(2)}) collective-permute-start(f32[64,128]{1,0:T(8,128)S(1)} %get-tuple-element.9), channel_id=1, source_target_pairs={{0,2},{2,0},{4,6},{6,4},{1,7},{7,1},{3,5},{5,3},{8,10},{10,8},{12,... | collective-permute-start | bytes 98312 | tf_op jit(solution)/shard_map/ppermute | solution.py:326
  48.2 9.6 %collective-permute-start.1 = (f32[64,128]{1,0:T(8,128)S(1)}, f32[64,128]{1,0:T(8,128)S(1)}, u32[]{:S(2)}, u32[]{:S(2)}) collective-permute-start(f32[64,128]{1,0:T(8,128)S(1)} %add.7.refs_1_), channel_id=1, source_target_pairs={{0,6},{6,0},{2,4},{4,2},{1,3},{3,1},{5,7},{7,5},{8,14},{14,8},{10,... | collective-permute-start | bytes 98312 | tf_op jit(solution)/shard_map/ppermute | solution.py:329
  58.0 31.0 %copy-start = (bf16[512,128]{1,0:T(8,128)(2,1)S(1)}, bf16[512,128]{1,0:T(8,128)(2,1)}, u32[]{:S(2)}) copy-start(bf16[512,128]{1,0:T(8,128)(2,1)} %refs_1_.4) | copy-start | bytes 393220
  58.0 31.0 %copy-start.1 = (bf16[512,128]{1,0:T(8,128)(2,1)S(1)}, bf16[512,128]{1,0:T(8,128)(2,1)}, u32[]{:S(2)}) copy-start(bf16[512,128]{1,0:T(8,128)(2,1)} %refs_2_.5) | copy-start | bytes 393220
  58.0 31.0 %copy-start.2 = (bf16[512,128]{1,0:T(8,128)(2,1)S(1)}, bf16[512,128]{1,0:T(8,128)(2,1)}, u32[]{:S(2)}) copy-start(bf16[512,128]{1,0:T(8,128)(2,1)} %refs_3_.5) | copy-start | bytes 393220
  58.0 31.0 %copy-start.3 = (bf16[512,128]{1,0:T(8,128)(2,1)S(1)}, bf16[512,128]{1,0:T(8,128)(2,1)}, u32[]{:S(2)}) copy-start(bf16[512,128]{1,0:T(8,128)(2,1)} %refs_4_.5) | copy-start | bytes 393220

commit v8 on v5

--- a/solution.py
+++ b/solution.py
@@ -317,7 +317,9 @@
     recv = exchange(pack(place, query, key, value, taps, cotangent))
     spec, terms = forward(blocks, chunks, recv, first_fwd, twist, second_fwd, second_inv, first_inv)
     send = inverse(blocks, chunks, spec, twist, second_inv, first_inv)
-    terms = terms + lax.ppermute(terms, ("zh", "core"), by_core(PAIRS_NEAR, PAIRS_ROUND))
+    near = lax.ppermute(terms, ("zh", "core"), by_core(PAIRS_NEAR, PAIRS_ROUND))
+    near, send = lax.optimization_barrier((near, send))
+    terms = terms + near
     send = fill(blocks, chunks, send, terms, lax.ppermute(terms, ("zh", "core"), by_core(PAIRS_ROUND, PAIRS_NEAR)))
     back = exchange(send)
     scale = 1.0 / math.sqrt(float(blocks * length * lax.axis_size(("y", "zh", "core"))))

time: 90.3 us -> 90.3 us (level)
    ppermute x1, waiting for transfers between devices: 1.29 us -> 0.06 us  [on_device(): near = lax.ppermute(terms, ('zh', 'core'), by_core(PAIRS_NEAR, PAIRS_ROUND))]
    ppermute x1, waiting for transfers between devices: 0.77 us -> 1.99 us  [on_device(): lax.ppermute(terms, ('zh', 'core'), by_core(PAIRS_ROUND, PAIRS_NEAR))]
where the time goes in v8:
time: 90.3 us; the launch traced here: 90.1 us
  blocking collectives  64.9 us (72%)
  starting transfers between devices  17.1 us (19%)
  Pallas kernels  5.2 us (6%)
  waiting for transfers between devices  2.05 us (2%)
    all_to_all x2, blocking collectives, exchange(): return lax.all_to_all(flat, GROUP, 0, 0, tiled=True).reshape(shape)  64.9 us
    ppermute x1, starting transfers between devices, on_device(): near = lax.ppermute(terms, ('zh', 'core'), by_core(PAIRS_NEAR, PAIRS_ROUND))  9.76 us
    ppermute x1, starting transfers between devices, on_device(): lax.ppermute(terms, ('zh', 'core'), by_core(PAIRS_ROUND, PAIRS_NEAR))  7.3 us
    ppermute x1, waiting for transfers between devices, on_device(): lax.ppermute(terms, ('zh', 'core'), by_core(PAIRS_ROUND, PAIRS_NEAR))  1.99 us
  transfers between devices with their start and end apart: 2, of which 2 were waited for; matrix products, arithmetic and copies ran while one was open for 0% of the time, Pallas kernels for 1%

profile of v8, /device:TPU:1, one launch (start us, length us, event | category | flops | bytes accessed | tf_op | source)
XLA Modules:
  0.0 90.1 jit_solution(8582906973496480725)
XLA Ops:
  0.6 0.0 copy-start.4
  0.6 0.0 copy-start.5
  0.7 0.0 copy-start.6
  0.7 0.0 copy-start.7
  0.7 0.0 copy-start.8
  0.7 1.4 %pack.1 = f32[1152,128]{1,0:T(8,128)S(1)} custom-call(s32[1]{0:T(128)} %bitcast.refs_0_, bf16[512,128]{1,0:T(8,128)(2,1)} %refs_1_.5, bf16[512,128]{1,0:T(8,128)(2,1)} %refs_2_.5, bf16[512,128]{1,0:T(8,128)(2,1)} %refs_3_.5, f32[512,128]{1,0:T(8,128)} %refs_4_.3, bf16[512,128]{1,0:T(8,128)(2,1)} %refs_4_.4), custom_call_target="tpu_custom_call" | custom-call | tf_op jit(solution)/shard_map/pack/pallas_call | solution.py:232
  2.2 33.4 %all_to_all.10 = f32[128,1,1152]{2,1,0:T(1,128)S(1)} all-to-all(f32[128,1,1152]{2,1,0:T(1,128)S(1)} %bitcast.7), channel_id=1, replica_groups=mesh['ctx'=16,'y'=4,'zh'=4,'core'=2] {'ctx','y','core'}, dimensions={0} | all-to-all | bytes 1179648 | tf_op jit(solution)/shard_map/all_to_all | solution.py:306
  35.5 0.0 copy-done.4
  35.5 0.0 copy-done.5
  35.5 0.0 copy-done.6
  35.5 0.0 copy-done.7
  35.5 0.0 copy-done.8
  35.6 1.2 %forward.1 = (f32[1088,256]{1,0:T(8,128)S(1)}, f32[64,128]{1,0:T(8,128)S(1)}) custom-call(f32[1152,128]{1,0:T(8,128)S(1)} %bitcast.8, bf16[128,192]{1,0:T(8,128)(2,1)S(1)} %copy-done.7, f32[64,256]{1,0:T(8,128)S(1)} %copy-done.6, bf16[512,256]{1,0:T(8,128)(2,1)S(1)} %copy-done.5, bf16[512,256]{1,0:T(8,128)(2,1)S(1)} %copy-done.4, bf16[64,384]{1,0:T(8,128)(2,1)S(1)} %copy-done.8), custom_call_target="tpu_custom_call" | custom-call | tf_op jit(solution)/shard_map/forward/pallas_call | solution.py:246
  36.8 9.8 %collective-permute-start = (f32[64,128]{1,0:T(8,128)S(1)}, f32[64,128]{1,0:T(8,128)S(1)}, u32[]{:S(2)}, u32[]{:S(2)}) collective-permute-start(f32[64,128]{1,0:T(8,128)S(1)} %get-tuple-element.9), channel_id=1, source_target_pairs={{0,2},{2,0},{4,6},{6,4},{1,7},{7,1},{3,5},{5,3},{8,10},{10,8},{12,... | collective-permute-start | bytes 98312 | tf_op jit(solution)/shard_map/ppermute | solution.py:320
  46.6 1.2 %inverse.1.refs_0_ = f32[1024,128]{1,0:T(8,128)S(1)} custom-call(f32[1088,256]{1,0:T(8,128)S(1)} %get-tuple-element.10.refs_0_, f32[64,256]{1,0:T(8,128)S(1)} %copy-done.6, bf16[512,256]{1,0:T(8,128)(2,1)S(1)} %copy-done.4, bf16[64,384]{1,0:T(8,128)(2,1)S(1)} %copy-done.8), custom_call_target="tpu_custom_call" | custom-call | flops 1000000000 | bytes 4000000 | tf_op jit(solution)/shard_map/inverse/pallas_call | solution.py:262
  47.8 0.1 collective-permute-done
  47.8 7.3 %collective-permute-start.1 = (f32[64,128]{1,0:T(8,128)S(1)}, f32[64,128]{1,0:T(8,128)S(1)}, u32[]{:S(2)}, u32[]{:S(2)}) collective-permute-start(f32[64,128]{1,0:T(8,128)S(1)} %add.7.refs_1_), channel_id=1, source_target_pairs={{0,6},{6,0},{2,4},{4,2},{1,3},{3,1},{5,7},{7,5},{8,14},{14,8},{10,... | collective-permute-start | bytes 98312 | tf_op jit(solution)/shard_map/ppermute | solution.py:323
  55.2 2.0 %collective-permute-done.1.refs_2_ = f32[64,128]{1,0:T(8,128)S(1)} collective-permute-done((f32[64,128]{1,0:T(8,128)S(1)}, f32[64,128]{1,0:T(8,128)S(1)}, u32[]{:S(2)}, u32[]{:S(2)}) %collective-permute-start.1) | collective-permute-done | bytes 32800 | tf_op jit(solution)/shard_map/ppermute | solution.py:323
  57.1 0.2 fill.1
  57.4 0.0 copy-start
  57.4 0.0 copy-start.1
  57.4 0.0 copy-start.2
  57.4 0.0 copy-start.3
  57.4 31.5 %all_to_all.11 = f32[128,1,1536]{2,1,0:T(1,128)S(1)} all-to-all(f32[128,1,1536]{2,1,0:T(1,128)S(1)} %bitcast.6), channel_id=1, replica_groups=mesh['ctx'=16,'y'=4,'zh'=4,'core'=2] {'ctx','y','core'}, dimensions={0} | all-to-all | bytes 1572864 | tf_op jit(solution)/shard_map/all_to_all | solution.py:306
  88.9 0.0 copy-done
  88.9 0.0 copy-done.1
  88.9 0.0 copy-done.2
  88.9 0.0 copy-done.3
  89.0 1.1 %outputs.1 = (bf16[512,128]{1,0:T(8,128)(2,1)}, bf16[512,128]{1,0:T(8,128)(2,1)}, bf16[512,128]{1,0:T(8,128)(2,1)}, bf16[512,128]{1,0:T(8,128)(2,1)}, f32[512,128]{1,0:T(8,128)}) custom-call(f32[1536,128]{1,0:T(8,128)S(1)} %bitcast.5, bf16[512,128]{1,0:T(8,128)(2,1)S(1)} %copy-done, bf16[512,128]{1,0:T(8,128)(2,1)S(1)} %copy-done.1, ...), custom_call_target="tpu_custom_call" | custom-call | tf_op jit(solution)/shard_map/outputs/pallas_call | solution.py:289
  (1 shorter events, 0.0 us)
Async XLA Ops:
  0.6 34.9 %copy-start.4 = (bf16[512,256]{1,0:T(8,128)(2,1)S(1)}, bf16[512,256]{1,0:T(8,128)(2,1)}, u32[]{:S(2)}) copy-start(bf16[512,256]{1,0:T(8,128)(2,1)} %constant.24.clone.refs_4_.refs_2_) | copy-start | bytes 786436
  0.6 34.9 %copy-start.5 = (bf16[512,256]{1,0:T(8,128)(2,1)S(1)}, bf16[512,256]{1,0:T(8,128)(2,1)}, u32[]{:S(2)}) copy-start(bf16[512,256]{1,0:T(8,128)(2,1)} %constant.23.clone.refs_3_) | copy-start | bytes 786436
  0.7 34.9 %copy-start.6 = (f32[64,256]{1,0:T(8,128)S(1)}, f32[64,256]{1,0:T(8,128)}, u32[]{:S(2)}) copy-start(f32[64,256]{1,0:T(8,128)} %constant.22.clone.refs_2_.refs_1_) | copy-start | bytes 196612
  0.7 34.9 %copy-start.7 = (bf16[128,192]{1,0:T(8,128)(2,1)S(1)}, bf16[128,192]{1,0:T(8,128)(2,1)}, u32[]{:S(2)}) copy-start(bf16[128,192]{1,0:T(8,128)(2,1)} %constant.21.clone.refs_1_) | copy-start | bytes 147460
  0.7 34.9 %copy-start.8 = (bf16[64,384]{1,0:T(8,128)(2,1)S(1)}, bf16[64,384]{1,0:T(8,128)(2,1)}, u32[]{:S(2)}) copy-start(bf16[64,384]{1,0:T(8,128)(2,1)} %constant.25.clone.refs_5_.refs_3_) | copy-start | bytes 147460
  36.8 11.1 %collective-permute-start = (f32[64,128]{1,0:T(8,128)S(1)}, f32[64,128]{1,0:T(8,128)S(1)}, u32[]{:S(2)}, u32[]{:S(2)}) collective-permute-start(f32[64,128]{1,0:T(8,128)S(1)} %get-tuple-element.9), channel_id=1, source_target_pairs={{0,2},{2,0},{4,6},{6,4},{1,7},{7,1},{3,5},{5,3},{8,10},{10,8},{12,... | collective-permute-start | bytes 98312 | tf_op jit(solution)/shard_map/ppermute | solution.py:320
  47.8 9.3 %collective-permute-start.1 = (f32[64,128]{1,0:T(8,128)S(1)}, f32[64,128]{1,0:T(8,128)S(1)}, u32[]{:S(2)}, u32[]{:S(2)}) collective-permute-start(f32[64,128]{1,0:T(8,128)S(1)} %add.7.refs_1_), channel_id=1, source_target_pairs={{0,6},{6,0},{2,4},{4,2},{1,3},{3,1},{5,7},{7,5},{8,14},{14,8},{10,... | collective-permute-start | bytes 98312 | tf_op jit(solution)/shard_map/ppermute | solution.py:323
  57.4 31.6 %copy-start = (bf16[512,128]{1,0:T(8,128)(2,1)S(1)}, bf16[512,128]{1,0:T(8,128)(2,1)}, u32[]{:S(2)}) copy-start(bf16[512,128]{1,0:T(8,128)(2,1)} %refs_1_.5) | copy-start | bytes 393220
  57.4 31.6 %copy-start.1 = (bf16[512,128]{1,0:T(8,128)(2,1)S(1)}, bf16[512,128]{1,0:T(8,128)(2,1)}, u32[]{:S(2)}) copy-start(bf16[512,128]{1,0:T(8,128)(2,1)} %refs_2_.5) | copy-start | bytes 393220
  57.4 31.6 %copy-start.2 = (bf16[512,128]{1,0:T(8,128)(2,1)S(1)}, bf16[512,128]{1,0:T(8,128)(2,1)}, u32[]{:S(2)}) copy-start(bf16[512,128]{1,0:T(8,128)(2,1)} %refs_3_.5) | copy-start | bytes 393220
  57.4 31.6 %copy-start.3 = (bf16[512,128]{1,0:T(8,128)(2,1)S(1)}, bf16[512,128]{1,0:T(8,128)(2,1)}, u32[]{:S(2)}) copy-start(bf16[512,128]{1,0:T(8,128)(2,1)} %refs_4_.4) | copy-start | bytes 393220

commit v9 on v5

--- a/solution.py
+++ b/solution.py
@@ -117,8 +117,8 @@
         0,
     )
     signals = [read(column, signal) for signal in range(2) for column in range(columns)] + [taps]
-    for start in range(0, len(signals), 2):
-        group = signals[start : start + 2]
+    for start in range(0, len(signals), 4):
+        group = signals[start : start + 4]
         wide = jnp.concatenate(group, 1) if len(group) > 1 else group[0]
         high, low = split(wide)
         mixed = dot(first_ref[...], jnp.concatenate([high, low, high], 0))

time: 90.3 us -> 90.3 us (level)
  no operation moved by 1% of the time
where the time goes in v9:
time: 90.3 us; the launch traced here: 90.1 us
  blocking collectives  64.9 us (72%)
  starting transfers between devices  17.1 us (19%)
  Pallas kernels  5.2 us (6%)
  waiting for transfers between devices  2.05 us (2%)
    all_to_all x2, blocking collectives, exchange(): return lax.all_to_all(flat, GROUP, 0, 0, tiled=True).reshape(shape)  64.9 us
    ppermute x1, starting transfers between devices, on_device(): lax.ppermute(terms, ('zh', 'core'), by_core(PAIRS_NEAR, PAIRS_ROUND))  9.76 us
    ppermute x1, starting transfers between devices, on_device(): lax.ppermute(terms, ('zh', 'core'), by_core(PAIRS_ROUND, PAIRS_NEAR))  7.3 us
  transfers between devices with their start and end apart: 2, of which 2 were waited for; matrix products, arithmetic and copies ran while one was open for 0% of the time, Pallas kernels for 1%

profile of v9, /device:TPU:1, one launch (start us, length us, event | category | flops | bytes accessed | tf_op | source)
XLA Modules:
  0.0 90.1 jit_solution(17595916564211988875)
XLA Ops:
  0.6 0.0 copy-start.4
  0.6 0.0 copy-start.5
  0.7 0.0 copy-start.6
  0.7 0.0 copy-start.7
  0.7 0.0 copy-start.8
  0.7 1.4 %pack.1 = f32[1152,128]{1,0:T(8,128)S(1)} custom-call(s32[1]{0:T(128)} %bitcast.refs_0_, bf16[512,128]{1,0:T(8,128)(2,1)} %refs_1_.5, bf16[512,128]{1,0:T(8,128)(2,1)} %refs_2_.5, bf16[512,128]{1,0:T(8,128)(2,1)} %refs_3_.5, f32[512,128]{1,0:T(8,128)} %refs_4_.3, bf16[512,128]{1,0:T(8,128)(2,1)} %refs_4_.4), custom_call_target="tpu_custom_call" | custom-call | tf_op jit(solution)/shard_map/pack/pallas_call | solution.py:232
  2.2 33.4 %all_to_all.10 = f32[128,1,1152]{2,1,0:T(1,128)S(1)} all-to-all(f32[128,1,1152]{2,1,0:T(1,128)S(1)} %bitcast.7), channel_id=1, replica_groups=mesh['ctx'=16,'y'=4,'zh'=4,'core'=2] {'ctx','y','core'}, dimensions={0} | all-to-all | bytes 1179648 | tf_op jit(solution)/shard_map/all_to_all | solution.py:306
  35.5 0.0 copy-done.4
  35.5 0.0 copy-done.5
  35.5 0.0 copy-done.6
  35.5 0.0 copy-done.7
  35.5 0.0 copy-done.8
  35.6 1.2 %forward.1 = (f32[1088,256]{1,0:T(8,128)S(1)}, f32[64,128]{1,0:T(8,128)S(1)}) custom-call(f32[1152,128]{1,0:T(8,128)S(1)} %bitcast.8, bf16[128,192]{1,0:T(8,128)(2,1)S(1)} %copy-done.7, f32[64,256]{1,0:T(8,128)S(1)} %copy-done.6, bf16[512,256]{1,0:T(8,128)(2,1)S(1)} %copy-done.5, bf16[512,256]{1,0:T(8,128)(2,1)S(1)} %copy-done.4, bf16[64,384]{1,0:T(8,128)(2,1)S(1)} %copy-done.8), custom_call_target="tpu_custom_call" | custom-call | tf_op jit(solution)/shard_map/forward/pallas_call | solution.py:246
  36.8 9.8 %collective-permute-start = (f32[64,128]{1,0:T(8,128)S(1)}, f32[64,128]{1,0:T(8,128)S(1)}, u32[]{:S(2)}, u32[]{:S(2)}) collective-permute-start(f32[64,128]{1,0:T(8,128)S(1)} %get-tuple-element.8), channel_id=1, source_target_pairs={{0,2},{2,0},{4,6},{6,4},{1,7},{7,1},{3,5},{5,3},{8,10},{10,8},{12,... | collective-permute-start | bytes 98312 | tf_op jit(solution)/shard_map/ppermute | solution.py:320
  46.6 1.3 %collective-permute-done = f32[64,128]{1,0:T(8,128)S(1)} collective-permute-done((f32[64,128]{1,0:T(8,128)S(1)}, f32[64,128]{1,0:T(8,128)S(1)}, u32[]{:S(2)}, u32[]{:S(2)}) %collective-permute-start) | collective-permute-done | bytes 32800 | tf_op jit(solution)/shard_map/ppermute | solution.py:320
  47.9 7.3 %collective-permute-start.1 = (f32[64,128]{1,0:T(8,128)S(1)}, f32[64,128]{1,0:T(8,128)S(1)}, u32[]{:S(2)}, u32[]{:S(2)}) collective-permute-start(f32[64,128]{1,0:T(8,128)S(1)} %add.7.refs_1_), channel_id=1, source_target_pairs={{0,6},{6,0},{2,4},{4,2},{1,3},{3,1},{5,7},{7,5},{8,14},{14,8},{10,... | collective-permute-start | bytes 98312 | tf_op jit(solution)/shard_map/ppermute | solution.py:321
  55.2 1.2 %inverse.1.refs_0_ = f32[1024,128]{1,0:T(8,128)S(1)} custom-call(f32[1088,256]{1,0:T(8,128)S(1)} %get-tuple-element.7.refs_0_, f32[64,256]{1,0:T(8,128)S(1)} %copy-done.6, bf16[512,256]{1,0:T(8,128)(2,1)S(1)} %copy-done.4, bf16[64,384]{1,0:T(8,128)(2,1)S(1)} %copy-done.8), custom_call_target="tpu_custom_call" | custom-call | flops 1000000000 | bytes 4000000 | tf_op jit(solution)/shard_map/inverse/pallas_call | solution.py:262
  56.4 0.8 collective-permute-done.1.refs_2_
  57.2 0.2 fill.1
  57.4 0.0 copy-start
  57.4 0.0 copy-start.1
  57.4 0.0 copy-start.2
  57.4 0.0 copy-start.3
  57.4 31.5 %all_to_all.11 = f32[128,1,1536]{2,1,0:T(1,128)S(1)} all-to-all(f32[128,1,1536]{2,1,0:T(1,128)S(1)} %bitcast.6), channel_id=1, replica_groups=mesh['ctx'=16,'y'=4,'zh'=4,'core'=2] {'ctx','y','core'}, dimensions={0} | all-to-all | bytes 1572864 | tf_op jit(solution)/shard_map/all_to_all | solution.py:306
  88.9 0.0 copy-done
  88.9 0.0 copy-done.1
  88.9 0.0 copy-done.2
  89.0 0.0 copy-done.3
  89.0 1.1 %outputs.1 = (bf16[512,128]{1,0:T(8,128)(2,1)}, bf16[512,128]{1,0:T(8,128)(2,1)}, bf16[512,128]{1,0:T(8,128)(2,1)}, bf16[512,128]{1,0:T(8,128)(2,1)}, f32[512,128]{1,0:T(8,128)}) custom-call(f32[1536,128]{1,0:T(8,128)S(1)} %bitcast.5, bf16[512,128]{1,0:T(8,128)(2,1)S(1)} %copy-done, bf16[512,128]{1,0:T(8,128)(2,1)S(1)} %copy-done.1, ...), custom_call_target="tpu_custom_call" | custom-call | tf_op jit(solution)/shard_map/outputs/pallas_call | solution.py:289
  (1 shorter events, 0.0 us)
Async XLA Ops:
  0.6 34.9 %copy-start.4 = (bf16[512,256]{1,0:T(8,128)(2,1)S(1)}, bf16[512,256]{1,0:T(8,128)(2,1)}, u32[]{:S(2)}) copy-start(bf16[512,256]{1,0:T(8,128)(2,1)} %constant.24.clone.refs_4_.refs_2_) | copy-start | bytes 786436
  0.6 34.9 %copy-start.5 = (bf16[512,256]{1,0:T(8,128)(2,1)S(1)}, bf16[512,256]{1,0:T(8,128)(2,1)}, u32[]{:S(2)}) copy-start(bf16[512,256]{1,0:T(8,128)(2,1)} %constant.23.clone.refs_3_) | copy-start | bytes 786436
  0.7 34.9 %copy-start.6 = (f32[64,256]{1,0:T(8,128)S(1)}, f32[64,256]{1,0:T(8,128)}, u32[]{:S(2)}) copy-start(f32[64,256]{1,0:T(8,128)} %constant.22.clone.refs_2_.refs_1_) | copy-start | bytes 196612
  0.7 34.9 %copy-start.7 = (bf16[128,192]{1,0:T(8,128)(2,1)S(1)}, bf16[128,192]{1,0:T(8,128)(2,1)}, u32[]{:S(2)}) copy-start(bf16[128,192]{1,0:T(8,128)(2,1)} %constant.21.clone.refs_1_) | copy-start | bytes 147460
  0.7 34.9 %copy-start.8 = (bf16[64,384]{1,0:T(8,128)(2,1)S(1)}, bf16[64,384]{1,0:T(8,128)(2,1)}, u32[]{:S(2)}) copy-start(bf16[64,384]{1,0:T(8,128)(2,1)} %constant.25.clone.refs_5_.refs_3_) | copy-start | bytes 147460
  36.8 11.1 %collective-permute-start = (f32[64,128]{1,0:T(8,128)S(1)}, f32[64,128]{1,0:T(8,128)S(1)}, u32[]{:S(2)}, u32[]{:S(2)}) collective-permute-start(f32[64,128]{1,0:T(8,128)S(1)} %get-tuple-element.8), channel_id=1, source_target_pairs={{0,2},{2,0},{4,6},{6,4},{1,7},{7,1},{3,5},{5,3},{8,10},{10,8},{12,... | collective-permute-start | bytes 98312 | tf_op jit(solution)/shard_map/ppermute | solution.py:320
  47.9 9.3 %collective-permute-start.1 = (f32[64,128]{1,0:T(8,128)S(1)}, f32[64,128]{1,0:T(8,128)S(1)}, u32[]{:S(2)}, u32[]{:S(2)}) collective-permute-start(f32[64,128]{1,0:T(8,128)S(1)} %add.7.refs_1_), channel_id=1, source_target_pairs={{0,6},{6,0},{2,4},{4,2},{1,3},{3,1},{5,7},{7,5},{8,14},{14,8},{10,... | collective-permute-start | bytes 98312 | tf_op jit(solution)/shard_map/ppermute | solution.py:321
  57.4 31.6 %copy-start = (bf16[512,128]{1,0:T(8,128)(2,1)S(1)}, bf16[512,128]{1,0:T(8,128)(2,1)}, u32[]{:S(2)}) copy-start(bf16[512,128]{1,0:T(8,128)(2,1)} %refs_1_.5) | copy-start | bytes 393220
  57.4 31.6 %copy-start.1 = (bf16[512,128]{1,0:T(8,128)(2,1)S(1)}, bf16[512,128]{1,0:T(8,128)(2,1)}, u32[]{:S(2)}) copy-start(bf16[512,128]{1,0:T(8,128)(2,1)} %refs_2_.5) | copy-start | bytes 393220
  57.4 31.6 %copy-start.2 = (bf16[512,128]{1,0:T(8,128)(2,1)S(1)}, bf16[512,128]{1,0:T(8,128)(2,1)}, u32[]{:S(2)}) copy-start(bf16[512,128]{1,0:T(8,128)(2,1)} %refs_3_.5) | copy-start | bytes 393220
  57.4 31.6 %copy-start.3 = (bf16[512,128]{1,0:T(8,128)(2,1)S(1)}, bf16[512,128]{1,0:T(8,128)(2,1)}, u32[]{:S(2)}) copy-start(bf16[512,128]{1,0:T(8,128)(2,1)} %refs_4_.4) | copy-start | bytes 393220
